TPU v7x, 512 devices: a whole 4x8x8 slice. The times are simulated.
512 devices in a mesh: lat: 32 (over y, z_lo, core), lon: 16 (over z_hi, x).
Axes of the slice: x: 4, y: 8, z: 8 (z_hi: 4, z_lo: 2; z = z_hi * 2 + z_lo), core: 2. Of those that a mesh axis runs over, the one named last changes fastest.
Arguments:
- adj_u: float32 [16, 2048, 2048], P(None, 'lat', 'lon'), may hold values from -6 to 6
- adj_v: float32 [16, 2048, 2048], P(None, 'lat', 'lon'), may hold values from -6 to 6
- adj_theta: float32 [16, 2048, 2048], P(None, 'lat', 'lon'), may hold values from -6 to 6
- adj_thick: float32 [16, 2048, 2048], P(None, 'lat', 'lon'), may hold values from -6 to 6
- theta_traj: float32 [16, 2048, 2048], P(None, 'lat', 'lon'), may hold values from 0.8 to 1.6
- dp_traj: float32 [16, 2048, 2048], P(None, 'lat', 'lon'), may hold values from 0.5 to 1.5
- cutoff: int32 [2048], replicated, may hold values from 32 to 511
- polar_flags: int32 [2048], replicated, may hold values from 0 to 1, as said below
Outputs:
- u_adjoint: float32 [16, 2048, 2048], P(None, 'lat', 'lon')
- v_adjoint: float32 [16, 2048, 2048], P(None, 'lat', 'lon')
- theta_adjoint: float32 [16, 2048, 2048], P(None, 'lat', 'lon')
- thickness_adjoint: float32 [16, 2048, 2048], P(None, 'lat', 'lon')
Inputs may be any that keep to these rules, and one draw needn't show every extreme that they name: polar_flags is 1 on the first S rows and the last N rows and 0 between; S and N lie between 256 and 512, and one of them equals 512.
All inputs are finite; a program needn't handle non-finite values.
Results may differ from a plain program's by a relative error of at most 0.00011.
Values sent between devices are 32-bit elements; how exact they have to be, the bound alone decides.
No kernel may reach another device: no remote copies, remote signals or barrier semaphores. Data moves between devices by JAX's collectives and lax.ppermute only.
A program may use at most 64 MiB of HBM per device.

v0:
```python
import jax
import jax.numpy as jnp
from jax import lax
from jax.sharding import PartitionSpec as P

KAPPA = 0.3
CROSS = 0.2
MERID = 0.3
HIGHEST = lax.Precision.HIGHEST


def extended(x, sides, width, wrap):
    for axis, dim in sides:
        size, length = (lax.axis_size(axis), x.shape[dim])
        up = [(i, (i + 1) % size) for i in range(size if wrap else size - 1)]
        down = [(j, i) for i, j in up]
        last = lax.slice_in_dim(x, length - width, length, axis=dim)
        initial = lax.slice_in_dim(x, 0, width, axis=dim)
        before = lax.ppermute(last, axis, up)
        after = lax.ppermute(initial, axis, down)
        x = jnp.concatenate([before, x, after], axis=dim)
    return x


def row_geometry(row_index, total_rows):
    position = row_index.astype(jnp.float32)
    centre = jnp.pi * ((position + 0.5) / total_rows - 0.5)
    face = jnp.pi * ((position + 1.0) / total_rows - 0.5)
    return (jnp.cos(face), 1.0 / (jnp.cos(centre) + 0.25))


def split_length(length):
    least = min(128, length)
    long_side = min(
        (d for d in range(1, length + 1) if length % d == 0 and d * d >= length and (d >= least))
    )
    return (length // long_side, long_side)


def phase_tables(first_count, second_count, modulus):
    first_index = jnp.arange(first_count, dtype=jnp.int32)
    second_index = jnp.arange(second_count, dtype=jnp.int32)
    phase = first_index[:, None] * second_index[None, :] % modulus
    angle = 2.0 * jnp.pi / modulus * phase.astype(jnp.float32)
    return (jnp.cos(angle), jnp.sin(angle))


def spectral_weights(cutoff_rows, short_side, long_side):
    length = short_side * long_side
    first_index = jnp.arange(short_side, dtype=jnp.int32)
    second_index = jnp.arange(long_side, dtype=jnp.int32)
    wave_index = first_index[:, None] + short_side * second_index[None, :]
    folded = jnp.minimum(wave_index, length - wave_index)
    wave = folded.astype(jnp.float32)[None]
    limit = cutoff_rows.astype(jnp.float32)[:, None, None]
    damping = jnp.where(wave < limit, 1.0, (limit / jnp.maximum(wave, 1.0)) ** 2)
    damping = jnp.where(folded[None] < length // 2, damping, 0.0)
    return damping / length


def filter_circles(circles, cutoff_rows):
    fields, rows, length = circles.shape
    short_side, long_side = split_length(length)
    cos_short, sin_short = phase_tables(short_side, short_side, short_side)
    cos_long, sin_long = phase_tables(long_side, long_side, long_side)
    cos_twist, sin_twist = phase_tables(short_side, long_side, length)
    weights = spectral_weights(cutoff_rows, short_side, long_side)[None]
    blocks = circles.reshape(fields, rows, short_side, long_side)
    first_re = jnp.einsum("krab,ac->krcb", blocks, cos_short, precision=HIGHEST)
    first_im = -jnp.einsum("krab,ac->krcb", blocks, sin_short, precision=HIGHEST)
    turned_re = first_re * cos_twist + first_im * sin_twist
    turned_im = first_im * cos_twist - first_re * sin_twist
    modes_re = jnp.einsum("krcb,bd->krcd", turned_re, cos_long, precision=HIGHEST) + jnp.einsum(
        "krcb,bd->krcd", turned_im, sin_long, precision=HIGHEST
    )
    modes_im = jnp.einsum("krcb,bd->krcd", turned_im, cos_long, precision=HIGHEST) - jnp.einsum(
        "krcb,bd->krcd", turned_re, sin_long, precision=HIGHEST
    )
    modes_re = modes_re * weights
    modes_im = modes_im * weights
    back_re = jnp.einsum("krcd,bd->krcb", modes_re, cos_long, precision=HIGHEST) - jnp.einsum(
        "krcd,bd->krcb", modes_im, sin_long, precision=HIGHEST
    )
    back_im = jnp.einsum("krcd,bd->krcb", modes_re, sin_long, precision=HIGHEST) + jnp.einsum(
        "krcd,bd->krcb", modes_im, cos_long, precision=HIGHEST
    )
    untwist_re = back_re * cos_twist - back_im * sin_twist
    untwist_im = back_re * sin_twist + back_im * cos_twist
    values = jnp.einsum("krcb,ac->krab", untwist_re, cos_short, precision=HIGHEST) - jnp.einsum(
        "krcb,ac->krab", untwist_im, sin_short, precision=HIGHEST
    )
    return values.reshape(fields, rows, length)


def polar_filter(winds, cutoff_rows, flag_rows):
    circles = lax.all_to_all(winds, "lon", split_axis=0, concat_axis=2, tiled=True)
    smooth_circles = filter_circles(circles, cutoff_rows)
    smoothed = lax.all_to_all(smooth_circles, "lon", split_axis=2, concat_axis=0, tiled=True)
    return jnp.where(flag_rows[None, :, None] > 0, smoothed, winds)


def shards(adj_u, adj_v, adj_theta, adj_thick, theta_traj, dp_traj, cutoff, polar_flags):
    levels, rows, width = adj_u.shape
    bands = lax.axis_size("lat")
    band = lax.axis_index("lat")
    total_rows = rows * bands
    own_cut = lax.dynamic_slice_in_dim(cutoff, band * rows, rows)
    own_flag = lax.dynamic_slice_in_dim(polar_flags, band * rows, rows)
    smoothed = polar_filter(jnp.concatenate([adj_u, adj_v], axis=0), own_cut, own_flag)
    wind_u = smoothed[:levels]
    wind_v = smoothed[levels:]
    stacked = jnp.stack([wind_u, wind_v, adj_thick, adj_theta, theta_traj, dp_traj])
    widened = extended(stacked, (("lon", 3),), 1, True)
    framed = extended(widened, (("lat", 2),), 1, False)
    u_frame = framed[0]
    v_frame = framed[1]
    thick_frame = framed[2]
    theta_frame = framed[3]
    traj_frame = framed[4]
    depth_frame = framed[5]
    row_index = band * rows - 1 + jnp.arange(rows + 2, dtype=jnp.int32)
    face_cos, metric = row_geometry(row_index, total_rows)
    face_cos = face_cos[None, :, None]
    metric = metric[None, :, None]
    inside = (row_index >= 0) & (row_index < total_rows)
    geo_adjoint = CROSS * metric[:, 1:] * (u_frame[:, 1:, 1:] - u_frame[:, 1:, :-1]) + MERID * (
        v_frame[:, 1:, 1:] - v_frame[:, :-1, 1:]
    )
    depth = depth_frame[:, 1:, 1:]
    traj_part = traj_frame[:, 1:, 1:]
    safe_depth = jnp.where(inside[None, 1:, None], depth, 1.0)
    thick_new = thick_frame[:, 1:, 1:] + traj_part * geo_adjoint
    theta_new = theta_frame[:, 1:, 1:] + depth * geo_adjoint
    change = thick_new + KAPPA * traj_part / safe_depth * theta_new
    flux_x = CROSS * metric[:, 1 : rows + 1] * (change[:, :rows, 1:] - change[:, :rows, :width])
    flux_y = MERID * (
        metric[:, 2:] * change[:, 1:, :width] - metric[:, 1 : rows + 1] * change[:, :rows, :width]
    )
    depth_x = 0.5 * (depth_frame[:, 1 : rows + 1, 1 : width + 1] + depth_frame[:, 1 : rows + 1, 2:])
    depth_y = 0.5 * (
        depth_frame[:, 1 : rows + 1, 1 : width + 1] + depth_frame[:, 2:, 1 : width + 1]
    )
    u_adjoint = wind_u + depth_x * flux_x
    v_adjoint = wind_v + depth_y * face_cos[:, 1 : rows + 1] * flux_y
    return (u_adjoint, v_adjoint, theta_new[:, :rows, :width], thick_new[:, :rows, :width])


def solution(mesh):
    in_specs = (
        P(None, "lat", "lon"),
        P(None, "lat", "lon"),
        P(None, "lat", "lon"),
        P(None, "lat", "lon"),
        P(None, "lat", "lon"),
        P(None, "lat", "lon"),
        P(),
        P(),
    )
    out_specs = (
        P(None, "lat", "lon"),
        P(None, "lat", "lon"),
        P(None, "lat", "lon"),
        P(None, "lat", "lon"),
    )
    return jax.shard_map(shards, mesh=mesh, in_specs=in_specs, out_specs=out_specs, check_vma=False)
```

profile of v0, /device:TPU:1, one launch (start us, length us, event | category | flops | bytes accessed | tf_op | source)
XLA Modules:
  0.0 151.1 jit_solution(9229780810935066804)
XLA Ops:
  0.6 2.0 %constant_dynamic-update-slice_fusion.1 = f32[32,64,128]{2,1,0:T(8,128)} fusion(f32[16,64,128]{2,1,0:T(8,128)} %param.8), kind=kLoop, calls=%fused_computation.97 | loop fusion | bytes 1048576
  3.4 13.4 %all-to-all-start = ((f32[32,64,128]{2,1,0:T(8,128)}), f32[32,64,128]{2,1,0:T(8,128)S(1)}, u32[]{:S(2)}, u32[]{:S(2)}) async-start(f32[32,64,128]{2,1,0:T(8,128)} %constant_dynamic-update-slice_fusion), calls=%async_computation | async-start | bytes 2097152 | tf_op jit(solution)/shard_map/all_to_all | solution.py:96
  17.9 20.7 %all-to-all-done = f32[32,64,128]{2,1,0:T(8,128)S(1)} async-done(((f32[32,64,128]{2,1,0:T(8,128)}), f32[32,64,128]{2,1,0:T(8,128)S(1)}, u32[]{:S(2)}, u32[]{:S(2)}) %all-to-all-start) | async-done | bytes 1048608 | tf_op jit(solution)/shard_map/all_to_all | solution.py:96
  38.7 1.5 %convolution_negate_fusion = f32[16,2,64,128]{3,0,2,1:T(8,128)S(1)} fusion(f32[16,2,64,128]{3,2,1,0:T(8,128)S(1)} %bitcast.102), kind=kOutput, calls=%fused_computation.9 | convolution fusion | flops 50597376 | bytes 2097152 | tf_op jit(solution)/shard_map/krab,ac->krcb/dot_general | solution.py:70
  40.2 1.5 %fusion.13 = f32[16,2,64,128]{3,0,2,1:T(8,128)S(1)} fusion(f32[16,2,64,128]{3,2,1,0:T(8,128)S(1)} %bitcast.103), kind=kOutput, calls=%fused_computation.32 | convolution fusion | flops 50335232 | bytes 2097152 | tf_op jit(solution)/shard_map/krab,ac->krcb/dot_general | solution.py:69
  55.1 3.2 %reshape.183 = f32[16,1,16384]{2,1,0:T(1,128)} reshape(f32[2048,2,64]{2,1,0:T(2,128)S(1)} %bitcast.104) | data formatting | bytes 2097152
  58.3 5.9 %all-to-all-start.1 = ((f32[16,1,16384]{2,1,0:T(1,128)}), f32[16,1,16384]{2,1,0:T(1,128)S(1)}, u32[]{:S(2)}, u32[]{:S(2)}) async-start(f32[16,1,16384]{2,1,0:T(1,128)} %reshape.183), calls=%async_computation.1 | async-start | bytes 2097152 | tf_op jit(solution)/shard_map/all_to_all | solution.py:98
  65.2 15.5 %all-to-all-done.1 = f32[16,1,16384]{2,1,0:T(1,128)S(1)} async-done(((f32[16,1,16384]{2,1,0:T(1,128)}), f32[16,1,16384]{2,1,0:T(1,128)S(1)}, u32[]{:S(2)}, u32[]{:S(2)}) %all-to-all-start.1) | async-done | bytes 1048608 | tf_op jit(solution)/shard_map/all_to_all | solution.py:98
  81.2 3.1 %reduce = f32[16,16384]{1,0:T(8,128)S(1)} reduce(f32[16,1,16384]{2,1,0:T(1,128)S(1)} %all-to-all-done.1, f32[]{:T(128)} %broadcast.353), dimensions={1}, to_apply=%all_to_all.27.reduce_sub_computation | reduce | bytes 2097156 | tf_op jit(solution)/shard_map/all_to_all | solution.py:98
  84.4 1.5 %reshape.184 = f32[2048,2,64]{2,1,0:T(2,128)S(1)} reshape(f32[16,16384]{1,0:T(8,128)S(1)} %reduce) | data formatting | bytes 2097152
  90.9 3.8 %fusion.140 = (f32[6,16,64,1]{3,2,1,0:T(8,128)}, f32[6,16,64,1]{3,2,1,0:T(8,128)}) fusion(f32[6,16,64,128]{3,2,1,0:T(8,128)S(1)} %bitcast_dynamic-update-slice_fusion), kind=kLoop, calls=%fused_computation.188 | loop fusion | bytes 98304 | tf_op jit(solution)/shard_map/slice | solution.py:17
  94.7 2.5 %copy.24 = f32[6,16,64,1]{2,1,3,0:T(8,128)S(1)} copy(f32[6,16,64,1]{3,2,1,0:T(8,128)} %get-tuple-element.17) | data formatting | bytes 49152 | tf_op jit(solution)/shard_map/slice | solution.py:17
  97.1 2.2 %collective-permute-start = (f32[6,16,64,1]{2,1,3,0:T(8,128)S(1)}, f32[6,16,64,1]{2,1,3,0:T(8,128)S(1)}, u32[]{:S(2)}, u32[]{:S(2)}) collective-permute-start(f32[6,16,64,1]{2,1,3,0:T(8,128)S(1)} %copy.24), channel_id=1, source_target_pairs={{0,1},{1,2},{2,3},{3,4},{4,5},{5,6},{6,7},{7,8},{8,9},{9,10},{10,1... | collective-permute-start | bytes 73736 | tf_op jit(solution)/shard_map/ppermute | solution.py:19
  99.4 2.5 %copy.25 = f32[6,16,64,1]{2,1,3,0:T(8,128)S(1)} copy(f32[6,16,64,1]{3,2,1,0:T(8,128)} %get-tuple-element.18) | data formatting | bytes 49152 | tf_op jit(solution)/shard_map/slice | solution.py:18
  101.8 7.3 %collective-permute-start.1 = (f32[6,16,64,1]{2,1,3,0:T(8,128)S(1)}, f32[6,16,64,1]{2,1,3,0:T(8,128)S(1)}, u32[]{:S(2)}, u32[]{:S(2)}) collective-permute-start(f32[6,16,64,1]{2,1,3,0:T(8,128)S(1)} %copy.25), channel_id=1, source_target_pairs={{1,0},{2,1},{3,2},{4,3},{5,4},{6,5},{7,6},{8,7},{9,8},{10,9},{11,1... | collective-permute-start | bytes 73736 | tf_op jit(solution)/shard_map/ppermute | solution.py:20
  109.2 2.3 %copy.26 = f32[6,16,64,1]{3,2,1,0:T(8,128)} copy(f32[6,16,64,1]{2,1,3,0:T(8,128)S(1)} %collective-permute-done) | data formatting | bytes 49152 | tf_op jit(solution)/shard_map/ppermute | solution.py:19
  111.5 2.2 %copy.27 = f32[6,16,64,1]{3,2,1,0:T(8,128)} copy(f32[6,16,64,1]{2,1,3,0:T(8,128)S(1)} %collective-permute-done.1) | data formatting | bytes 49152 | tf_op jit(solution)/shard_map/ppermute | solution.py:20
  113.8 2.2 %pad_maximum_fusion.3 = (f32[6,16,1,130]{3,2,1,0:T(1,128)S(1)}, f32[6,16,1,130]{3,2,1,0:T(1,128)S(1)}) fusion(f32[6,16,64,1]{3,2,1,0:T(8,128)} %copy.27, f32[6,16,64,128]{3,2,1,0:T(8,128)S(1)} %bitcast_dynamic-update-slice_fusion, f32[6,16,64,1]{3,2,1,0:T(8,128)} %copy.26), kind=kLoop, calls=%fused_computation.74 | loop fusion | flops 49920 | bytes 3294720 | tf_op jit(solution)/shard_map/slice | solution.py:17
  116.0 19.3 %collective-permute-start.2 = (f32[6,16,1,130]{3,2,1,0:T(1,128)S(1)}, f32[6,16,1,130]{3,2,1,0:T(1,128)S(1)}, u32[]{:S(2)}, u32[]{:S(2)}) collective-permute-start(f32[6,16,1,130]{3,2,1,0:T(1,128)S(1)} %get-tuple-element.7), channel_id=1, source_target_pairs={{0,16},{16,32},{32,48},{48,64},{64,80},{80,96},{96,112},{112,128},... | collective-permute-start | bytes 149768 | tf_op jit(solution)/shard_map/ppermute | solution.py:19
  135.2 1.9 %collective-permute-start.3 = (f32[6,16,1,130]{3,2,1,0:T(1,128)S(1)}, f32[6,16,1,130]{3,2,1,0:T(1,128)S(1)}, u32[]{:S(2)}, u32[]{:S(2)}) collective-permute-start(f32[6,16,1,130]{3,2,1,0:T(1,128)S(1)} %get-tuple-element.8), channel_id=1, source_target_pairs={{16,0},{32,16},{48,32},{64,48},{80,64},{96,80},{112,96},{128,112},... | collective-permute-start | bytes 149768 | tf_op jit(solution)/shard_map/ppermute | solution.py:20
  137.2 3.9 %collective-permute-done.3 = f32[6,16,1,130]{3,2,1,0:T(1,128)S(1)} collective-permute-done((f32[6,16,1,130]{3,2,1,0:T(1,128)S(1)}, f32[6,16,1,130]{3,2,1,0:T(1,128)S(1)}, u32[]{:S(2)}, u32[]{:S(2)}) %collective-permute-start.3) | collective-permute-done | bytes 49952 | tf_op jit(solution)/shard_map/ppermute | solution.py:20
  141.2 3.5 %pad_maximum_fusion = f32[6,16,66,130]{3,2,1,0:T(8,128)S(1)} fusion(f32[6,16,1,130]{3,2,1,0:T(1,128)S(1)} %collective-permute-done.3, f32[6,16,64,1]{3,2,1,0:T(8,128)S(1)} %copy-done.1, f32[6,16,64,128]{3,2,1,0:T(8,128)S(1)} %bitcast_dynamic-update-slice_fusion, f32[6,16,64,1]{3,2,1,0:T(8,128)S(1)} %copy-done, f32[6,16,1,130]{3,2,1,0:T(1,128)S(1)} %collective-permute-done.2), kind=kLoop, calls=%fused_computation | loop fusion | flops 3294720 | bytes 6589440 | tf_op jit(solution)/shard_map/concatenate | solution.py:21
  145.4 2.3 %multiply_add_fusion = (f32[16,65,129]{2,1,0:T(8,128)S(1)}, f32[16,65,129]{2,1,0:T(8,128)S(1)}, f32[16,65,129]{2,1,0:T(8,128)S(1)}) fusion(f32[16,66,130]{2,1,0:T(8,128)S(1)} %get-tuple-element.14, f32[16,66,130]{2,1,0:T(8,128)S(1)} %get-tuple-element.13, pred[65]{0:T(512)(128)(4,1)S(1)} %slice.123, f32[16,66,130]{2,1,0:T(8,128)S(1)} %get-tuple-element.10, ...), kind=kLoop, calls=%fused_computation.23 | loop fusion | flops 1878240 | bytes 5903365 | tf_op jit(solution)/shard_map/add | solution.py:134
  149.5 1.6 %fusion.30 = (f32[16,64,128]{2,1,0:T(8,128)}, f32[16,64,128]{2,1,0:T(8,128)}) fusion(f32[16,65,129]{2,1,0:T(8,128)S(1)} %get-tuple-element.4, f32[16,66,130]{2,1,0:T(8,128)S(1)} %get-tuple-element.14, f32[32,64,128]{2,1,0:T(8,128)S(1)} %copy-done.3, f32[64]{0:T(128)S(1)} %get-tuple-element.20, f32[64]{0:T(128)S(1)} %get-tuple-element.19, ...), kind=kLoop, calls=%fused_computation.53 | loop fusion | flops 1835008 | bytes 5243904 | tf_op jit(solution)/shard_map/add | solution.py:144
  (59 shorter events, 24.2 us)
Async XLA Ops:
  0.6 2.0 %copy-start.4 = (f32[16,64,128]{2,1,0:T(8,128)S(1)}, f32[16,64,128]{2,1,0:T(8,128)}, u32[]{:S(2)}) copy-start(f32[16,64,128]{2,1,0:T(8,128)} %param.9) | copy-start | bytes 1572868
  3.4 35.2 %all-to-all-start = ((f32[32,64,128]{2,1,0:T(8,128)}), f32[32,64,128]{2,1,0:T(8,128)S(1)}, u32[]{:S(2)}, u32[]{:S(2)}) async-start(f32[32,64,128]{2,1,0:T(8,128)} %constant_dynamic-update-slice_fusion), calls=%async_computation | async-start | bytes 2097152 | tf_op jit(solution)/shard_map/all_to_all | solution.py:96
  58.3 22.4 %all-to-all-start.1 = ((f32[16,1,16384]{2,1,0:T(1,128)}), f32[16,1,16384]{2,1,0:T(1,128)S(1)}, u32[]{:S(2)}, u32[]{:S(2)}) async-start(f32[16,1,16384]{2,1,0:T(1,128)} %reshape.183), calls=%async_computation.1 | async-start | bytes 2097152 | tf_op jit(solution)/shard_map/all_to_all | solution.py:98
  88.2 1.5 copy-start.2
  88.2 1.4 copy-start.5
  88.3 1.5 %copy-start.6 = (f32[16,64,128]{2,1,0:T(8,128)S(1)}, f32[16,64,128]{2,1,0:T(8,128)}, u32[]{:S(2)}) copy-start(f32[16,64,128]{2,1,0:T(8,128)} %param.10) | copy-start | bytes 1572868
  89.7 1.1 copy-start.7
  89.8 1.1 copy-start.8
  97.1 12.1 %collective-permute-start = (f32[6,16,64,1]{2,1,3,0:T(8,128)S(1)}, f32[6,16,64,1]{2,1,3,0:T(8,128)S(1)}, u32[]{:S(2)}, u32[]{:S(2)}) collective-permute-start(f32[6,16,64,1]{2,1,3,0:T(8,128)S(1)} %copy.24), channel_id=1, source_target_pairs={{0,1},{1,2},{2,3},{3,4},{4,5},{5,6},{6,7},{7,8},{8,9},{9,10},{10,1... | collective-permute-start | bytes 73736 | tf_op jit(solution)/shard_map/ppermute | solution.py:19
  101.8 9.7 %collective-permute-start.1 = (f32[6,16,64,1]{2,1,3,0:T(8,128)S(1)}, f32[6,16,64,1]{2,1,3,0:T(8,128)S(1)}, u32[]{:S(2)}, u32[]{:S(2)}) collective-permute-start(f32[6,16,64,1]{2,1,3,0:T(8,128)S(1)} %copy.25), channel_id=1, source_target_pairs={{1,0},{2,1},{3,2},{4,3},{5,4},{6,5},{7,6},{8,7},{9,8},{10,9},{11,1... | collective-permute-start | bytes 73736 | tf_op jit(solution)/shard_map/ppermute | solution.py:20
  113.8 27.4 %copy-start = (f32[6,16,64,1]{3,2,1,0:T(8,128)S(1)}, f32[6,16,64,1]{3,2,1,0:T(8,128)}, u32[]{:S(2)}) copy-start(f32[6,16,64,1]{3,2,1,0:T(8,128)} %copy.26) | copy-start | bytes 73732
  113.8 27.4 %copy-start.1 = (f32[6,16,64,1]{3,2,1,0:T(8,128)S(1)}, f32[6,16,64,1]{3,2,1,0:T(8,128)}, u32[]{:S(2)}) copy-start(f32[6,16,64,1]{3,2,1,0:T(8,128)} %copy.27) | copy-start | bytes 73732
  116.0 21.3 %collective-permute-start.2 = (f32[6,16,1,130]{3,2,1,0:T(1,128)S(1)}, f32[6,16,1,130]{3,2,1,0:T(1,128)S(1)}, u32[]{:S(2)}, u32[]{:S(2)}) collective-permute-start(f32[6,16,1,130]{3,2,1,0:T(1,128)S(1)} %get-tuple-element.7), channel_id=1, source_target_pairs={{0,16},{16,32},{32,48},{48,64},{64,80},{80,96},{96,112},{112,128},... | collective-permute-start | bytes 149768 | tf_op jit(solution)/shard_map/ppermute | solution.py:19
  135.2 5.9 %collective-permute-start.3 = (f32[6,16,1,130]{3,2,1,0:T(1,128)S(1)}, f32[6,16,1,130]{3,2,1,0:T(1,128)S(1)}, u32[]{:S(2)}, u32[]{:S(2)}) collective-permute-start(f32[6,16,1,130]{3,2,1,0:T(1,128)S(1)} %get-tuple-element.8), channel_id=1, source_target_pairs={{16,0},{32,16},{48,32},{64,48},{80,64},{96,80},{112,96},{128,112},... | collective-permute-start | bytes 149768 | tf_op jit(solution)/shard_map/ppermute | solution.py:20
  147.8 1.7 %copy-start.3 = (f32[32,64,128]{2,1,0:T(8,128)S(1)}, f32[32,64,128]{2,1,0:T(8,128)}, u32[]{:S(2)}) copy-start(f32[32,64,128]{2,1,0:T(8,128)} %copy-done.2) | copy-start | bytes 3145732
where the time goes:
time: 152 us; the launch traced here: 151 us
  starting transfers between devices  50 us (33%)
  waiting for transfers between devices  40.1 us (26%)
  local copies, waits for them, and re-layouts  28.3 us (19%)
  other arithmetic  16.3 us (11%)
  matrix products  15.4 us (10%)
    ppermute x2, starting transfers between devices, extended(): before = lax.ppermute(last, axis, up)  21.5 us
    all_to_all x1, waiting for transfers between devices, polar_filter(): lax.all_to_all(winds, 'lon', split_axis=0, concat_axis=2, tiled=True)  20.7 us
    all_to_all x1, waiting for transfers between devices, polar_filter(): lax.all_to_all(smooth_circles, 'lon', split_axis=2, concat_axis=0, tiled=...  15.5 us
    all_to_all x1, starting transfers between devices, polar_filter(): lax.all_to_all(winds, 'lon', split_axis=0, concat_axis=2, tiled=True)  13.4 us
    unnamed x26, local copies, waits for them, and re-layouts  9.24 us
    ppermute x2, starting transfers between devices, extended(): after = lax.ppermute(initial, axis, down)  9.24 us
    slice x2, local copies, waits for them, and re-layouts, extended(): last = lax.slice_in_dim(x, length - width, length, axis=dim)  6.21 us
    all_to_all x1, starting transfers between devices, polar_filter(): lax.all_to_all(smooth_circles, 'lon', split_axis=2, concat_axis=0, tiled=...  5.92 us
  transfers between devices with their start and end apart: 6, of which 3 were waited for; matrix products, arithmetic and copies ran while one was open for 5% of the time, Pallas kernels for 0%

commit v1 on v0

v1 whole, which is shorter than its diff:
```python
import functools

import jax
import jax.numpy as jnp
import numpy as np
from jax import lax
from jax.experimental import pallas as pl
from jax.experimental.pallas import tpu as pltpu
from jax.sharding import PartitionSpec as P

KAPPA = 0.3
CROSS = 0.2
MERID = 0.3
LANES = 128
PAD_ROWS = 8
VMEM_LIMIT = 24 * 1024 * 1024
VMEM_LARGE = 56 * 1024 * 1024


def filter_tables(segments, width):
    length = segments * width
    half = segments // 2
    b = np.arange(width)
    angle = 2.0 * np.pi * (np.outer(b, b) % width) / width
    cos, sin = np.cos(angle), np.sin(angle)
    forward = np.block([[cos, -sin], [sin, cos]])
    n = np.arange(2 * width)
    real_angle = 2.0 * np.pi * (np.outer(n, np.arange(width + 1)) % (2 * width)) / (2 * width)
    real_forward = np.concatenate([np.cos(real_angle), -np.sin(real_angle[:, 1:width])], axis=1)
    twist = 2.0 * np.pi * np.outer(np.arange(1, half), b) / length
    twist_tables = np.stack([np.cos(twist), np.sin(twist)])
    waves = np.zeros((half, 2 * width))
    waves[0] = half * np.concatenate([np.arange(width + 1), np.arange(1, width)])
    for c in range(1, half):
        waves[c] = np.tile(c + segments * b, 2)
    folded = np.minimum(waves, length - waves)
    scale = np.where(folded < length // 2, 2.0 / length, 0.0)
    scale[0, 0] = 1.0 / length
    bound = scale / np.maximum(folded, 1.0) ** 2

    def split(matrix):
        matrix = matrix.astype(np.float32)
        high = matrix.astype(jnp.bfloat16)
        low = (matrix - high.astype(np.float32)).astype(jnp.bfloat16)
        return [jnp.asarray(high), jnp.asarray(low)]

    matrices = split(forward) + split(real_forward) + split(forward.T) + split(real_forward.T)
    return (
        matrices,
        jnp.asarray(twist_tables, jnp.float32),
        jnp.asarray(np.stack([scale, bound]), jnp.float32),
    )


def split_product(values, high_ref, low_ref):
    high = values.astype(jnp.bfloat16)
    low = (values - high.astype(jnp.float32)).astype(jnp.bfloat16)
    product = functools.partial(jnp.dot, preferred_element_type=jnp.float32)
    return (
        product(high, high_ref[...])
        + (product(low, high_ref[...]) + product(high, low_ref[...]))
    )


A1, B1, G1 = (float(np.cos(np.pi / 8)), float(np.cos(np.pi / 4)), float(np.cos(3 * np.pi / 8)))
ODD = {
    1: ((A1, B1, G1), (G1, B1, A1), 1.0),
    3: ((G1, -B1, -A1), (A1, B1, -G1), -1.0),
    5: ((-G1, -B1, A1), (A1, -B1, -G1), 1.0),
    7: ((-A1, B1, -G1), (G1, -B1, A1), -1.0),
}


def segment_transform(x):
    e = [x[j] + x[j + 8] for j in range(8)]
    o = [x[j] - x[j + 8] for j in range(8)]
    f = [e[j] + e[j + 4] for j in range(4)]
    g = [e[j] - e[j + 4] for j in range(4)]
    out = {4: (f[0] - f[2], f[3] - f[1])}
    minus, plus = B1 * (g[1] - g[3]), B1 * (g[1] + g[3])
    out[2] = (g[0] + minus, -g[2] - plus)
    out[6] = (g[0] - minus, g[2] - plus)
    d = [o[j] - o[8 - j] for j in (1, 2, 3)]
    s = [o[j] + o[8 - j] for j in (1, 2, 3)]
    for c, (cos, sin, sign) in ODD.items():
        real = o[0] + cos[0] * d[0] + cos[1] * d[1] + cos[2] * d[2]
        imag = -(sign * o[4] + sin[0] * s[0] + sin[1] * s[1] + sin[2] * s[2])
        out[c] = (real, imag)
    return (f[0] + f[2], f[1] + f[3]), out


def segment_inverse(even, odd, z):
    quarter = [z[4][0], -z[4][1], -z[4][0], z[4][1]]
    f = [(even if j % 2 == 0 else odd) + quarter[j] for j in range(4)]
    r_minus, i_minus = z[2][0] - z[6][0], z[6][1] - z[2][1]
    r_plus, i_plus = z[2][0] + z[6][0], z[2][1] + z[6][1]
    g = [r_plus, B1 * (r_minus - i_plus), i_minus, -B1 * (r_minus + i_plus)]
    e = [f[j] + g[j] for j in range(4)] + [f[j] - g[j] for j in range(4)]
    o = [None] * 8
    o[0] = z[1][0] + z[3][0] + z[5][0] + z[7][0]
    o[4] = -(z[1][1] - z[3][1] + z[5][1] - z[7][1])
    for j in (1, 2, 3):
        d = sum(ODD[c][0][j - 1] * z[c][0] for c in (1, 3, 5, 7))
        s = -sum(ODD[c][1][j - 1] * z[c][1] for c in (1, 3, 5, 7))
        o[j] = d + s
        o[8 - j] = s - d
    return [e[j] + o[j] for j in range(8)] + [e[j] - o[j] for j in range(8)]


def ceil_to(value, step):
    return -(-value // step) * step


def filter_body(x_ref, limit_ref, flag_ref, twist_ref, weight_ref, matrices, out_ref, work_ref):
    segments, rows, width = x_ref.shape
    half = segments // 2
    base = ceil_to((half - 1) * rows, 16)
    forward, forward_low, real, real_low, back, back_low, real_back, real_back_low = matrices
    group = PAD_ROWS

    @pl.loop(0, rows // group)
    def _(step):
        at = pl.multiple_of(step * group, group)
        here = pl.ds(at, group)
        (even, odd), classes = segment_transform([x_ref[a, here, :] for a in range(segments)])
        to = pl.ds(pl.multiple_of(base + at, group), group)
        work_ref[to, :width] = even
        work_ref[to, width:] = odd
        for c in range(1, half):
            re, im = classes[c]
            cos, sin = twist_ref[0, c - 1 : c, :], twist_ref[1, c - 1 : c, :]
            to = pl.ds(pl.multiple_of((c - 1) * rows + at, group), group)
            work_ref[to, :width] = re * cos + im * sin
            work_ref[to, width:] = im * cos - re * sin

    limit = limit_ref[...]
    limit = limit * limit
    limit = jnp.concatenate([limit, limit], axis=1)

    def weights(c):
        return jnp.minimum(weight_ref[0, c : c + 1, :], limit * weight_ref[1, c : c + 1, :])

    spectrum = split_product(work_ref[:base, :], forward, forward_low)
    damping = [weights(c) for c in range(1, half)]
    if base > (half - 1) * rows:
        damping.append(jnp.zeros((base - (half - 1) * rows, 2 * width), jnp.float32))
    spectrum = spectrum * jnp.concatenate(damping, axis=0)
    work_ref[:base, :] = split_product(spectrum, back, back_low)
    spectrum = split_product(work_ref[base : base + rows, :], real, real_low) * weights(0)
    work_ref[base : base + rows, :] = split_product(spectrum, real_back, real_back_low)

    @pl.loop(0, rows // group)
    def _(step):
        at = pl.multiple_of(step * group, group)
        here = pl.ds(at, group)
        first = pl.ds(pl.multiple_of(base + at, group), group)
        z = {}
        for c in range(1, half):
            cos, sin = twist_ref[0, c - 1 : c, :], twist_ref[1, c - 1 : c, :]
            frm = pl.ds(pl.multiple_of((c - 1) * rows + at, group), group)
            re, im = work_ref[frm, :width], work_ref[frm, width:]
            z[c] = (re * cos - im * sin, re * sin + im * cos)
        smooth = segment_inverse(work_ref[first, :width], work_ref[first, width:], z)
        flagged = flag_ref[here, :] > 0.0
        for a in range(segments):
            out_ref[a, here, :] = jnp.where(flagged, smooth[a], x_ref[a, here, :])


def lane_index(shape):
    return lax.broadcasted_iota(jnp.int32, shape, len(shape) - 1)


def gather_columns(out_ref, start, rows, picks):
    shape = (rows, LANES)
    lanes = lane_index(shape)
    total = jnp.zeros(shape, jnp.float32)
    for q, a, lane in picks:
        column = jnp.broadcast_to(out_ref[a, start : start + rows, lane : lane + 1], shape)
        total = jnp.where(lanes == q, column, total)
    return total


def edge_kernel(u_first_ref, v_first_ref, v_last_ref, north_ref, south_ref):
    north_ref[0] = u_first_ref[:, 0, :]
    north_ref[1] = v_first_ref[:, 0, :]
    south_ref[...] = v_last_ref[:, PAD_ROWS - 1, :]


def pair_kernel(u_ref, v_ref, south_ref, north_ref, out_ref):
    levels, rows, width = u_ref.shape
    main = 2 * rows
    out_ref[:, :rows, :] = u_ref[...]
    out_ref[:, rows:main, :] = v_ref[...]
    out_ref[:, main:, :] = jnp.zeros((levels, PAD_ROWS, width), jnp.float32)
    out_ref[:, main, :] = south_ref[...]
    out_ref[:, main + 1, :] = north_ref[1]
    out_ref[:, main + 2, :] = north_ref[0]


def rows_kernel(limits_ref, flags_ref, limit_block_ref, flag_block_ref, limit_out, flag_out):
    rows = (limit_out.shape[0] - PAD_ROWS) // 2
    count = limits_ref.shape[0]
    first = lax.axis_index("lat") * rows
    block, part = first // LANES, (first % LANES) // rows
    south, north = jnp.maximum(first - 1, 0), jnp.minimum(first + rows, count - 1)
    sub = lax.broadcasted_iota(jnp.int32, (PAD_ROWS, LANES), 0)
    for line_ref, scalar_ref, out_ref in (
        (limit_block_ref, limits_ref, limit_out),
        (flag_block_ref, flags_ref, flag_out),
    ):
        line = jnp.broadcast_to(line_ref[pl.ds(block, 1), :].astype(jnp.float32), (LANES, LANES)).T
        own = line[:rows]
        for p in range(1, LANES // rows):
            own = jnp.where(part == p, line[p * rows : (p + 1) * rows], own)
        out_ref[:rows, :] = own
        out_ref[rows : 2 * rows, :] = own
        tail = jnp.where(sub == 0, scalar_ref[south], scalar_ref[north])
        out_ref[2 * rows :, :] = tail.astype(jnp.float32)


def filter_kernel(x_ref, limit_ref, flag_ref, geo_ref, twist_ref, weight_ref, *rest):
    matrices, (out_ref, work_ref) = rest[:8], rest[8:]
    segments, tall, width = x_ref.shape
    main = tall - PAD_ROWS
    rows = main // 2
    metric = geo_ref[0, :rows, :]
    metric_north = geo_ref[0, rows : rows + 1, :]
    edge = lane_index((1, width)) == 0
    filter_body(x_ref, limit_ref, flag_ref, twist_ref, weight_ref, matrices, out_ref, work_ref)
    u_north = [out_ref[a, main + 2 : main + 3, :] for a in range(segments)]
    rolled = [pltpu.roll(u_north[a], 1, 1) for a in range(segments)]
    last = width - 1
    ahead = [(a, (a + 1) % segments, 0) for a in range(segments)]
    behind = [(segments + a, (a - 1) % segments, last) for a in range(segments)]
    own = [(a, a, last) for a in range(segments)]
    side = gather_columns(out_ref, 0, rows, ahead + behind) - gather_columns(out_ref, 0, rows, own)
    v_ahead = gather_columns(out_ref, rows, rows + 1, ahead)
    v_body = v_ahead[:rows]
    top = lax.broadcasted_iota(jnp.int32, (rows, LANES), 0) == 0
    v_south = jnp.where(top, v_ahead[rows : rows + 1], pltpu.roll(v_body, 1, 0))
    mixed = CROSS * metric * side + MERID * (v_body - v_south)
    columns = jnp.where(lane_index((rows, LANES)) < segments, mixed, side)
    columns = jnp.concatenate([columns, jnp.zeros((LANES - rows, LANES), jnp.float32)], axis=0).T
    for a in range(segments):
        west = jnp.where(edge, rolled[a - 1], rolled[a])
        north = CROSS * metric_north * (u_north[a] - west) + MERID * (
            out_ref[a, main + 1 : main + 2, :] - out_ref[a, main - 1 : main, :]
        )
        out_ref[a, main + 1 : main + 2, :] = north
        out_ref[a, main + 2 : main + 3, :] = columns[a : a + 1]
        out_ref[a, main + 3 : main + 4, :] = columns[segments + a : segments + a + 1]


def substep_kernel(
    winds_ref, thick_ref, theta_ref, traj_ref, depth_ref, geo_ref, north_ref, east_ref,
    u_out, v_out, theta_out, thick_out,
):
    levels, rows, width = thick_ref.shape
    main = 2 * rows
    metric, face = geo_ref[0, :rows, :], geo_ref[1, :rows, :]
    metric_north = geo_ref[0, rows : rows + 1, :]
    shape = (rows, width)
    lanes, sub = lane_index(shape), lax.broadcasted_iota(jnp.int32, shape, 0)
    first_lane, last_lane = lanes == 0, lanes == width - 1
    first_row, last_row = sub == 0, sub == rows - 1
    lines = []
    for k in range(levels):
        ga_east = winds_ref[k, main + 2 : main + 3, :]
        lines.append(east_ref[0, k : k + 1, :] + (1.0 + KAPPA) * east_ref[1, k : k + 1, :] * ga_east)
    for k in range(levels):
        lines.append(east_ref[2, k : k + 1, :])
    for k in range(levels):
        lines.append(winds_ref[k, main + 3 : main + 4, :])
    lines.append(jnp.zeros((LANES - 3 * levels, width), jnp.float32))
    columns = jnp.concatenate(lines, axis=0).T
    for k in range(levels):
        ua, va = winds_ref[k, :rows, :], winds_ref[k, rows:main, :]
        traj, depth = traj_ref[k], depth_ref[k]
        e_east = jnp.broadcast_to(columns[:rows, k : k + 1], shape)
        depth_east = jnp.broadcast_to(columns[:rows, levels + k : levels + k + 1], shape)
        u_west = jnp.broadcast_to(columns[:rows, 2 * levels + k : 2 * levels + k + 1], shape)
        west = jnp.where(first_lane, u_west, pltpu.roll(ua, 1, 1))
        south = jnp.where(first_row, winds_ref[k, main : main + 1, :], pltpu.roll(va, 1, 0))
        ga = CROSS * metric * (ua - west) + MERID * (va - south)
        thick = thick_ref[k] + traj * ga
        theta = theta_ref[k] + depth * ga
        e = thick + KAPPA * (traj / depth) * theta
        e_shift = jnp.where(last_lane, e_east, pltpu.roll(e, width - 1, 1))
        depth_shift = jnp.where(last_lane, depth_east, pltpu.roll(depth, width - 1, 1))
        u_out[k] = ua + (0.5 * CROSS) * (depth + depth_shift) * metric * (e_shift - e)
        e_north = north_ref[0, k : k + 1, :] + (1.0 + KAPPA) * north_ref[1, k : k + 1, :] * winds_ref[k, main + 1 : main + 2, :]
        me = metric * e
        me_shift = jnp.where(last_row, metric_north * e_north, pltpu.roll(me, rows - 1, 0))
        depth_up = jnp.where(last_row, north_ref[2, k : k + 1, :], pltpu.roll(depth, rows - 1, 0))
        v_out[k] = va + (0.5 * MERID) * (depth + depth_up) * face * (me_shift - me)
        theta_out[k] = theta
        thick_out[k] = thick


def row_geometry(row_index, total_rows):
    position = row_index.astype(jnp.float32)
    centre = jnp.pi * ((position + 0.5) / total_rows - 0.5)
    face = jnp.pi * ((position + 1.0) / total_rows - 0.5)
    return (jnp.cos(face), 1.0 / (jnp.cos(centre) + 0.25))


def spread(column):
    return jnp.broadcast_to(column[:, None], (column.shape[0], LANES))


def swap(blocks):
    return lax.all_to_all(blocks, "lon", split_axis=0, concat_axis=0, tiled=True)


def shards(adj_u, adj_v, adj_theta, adj_thick, theta_traj, dp_traj, cutoff, polar_flags):
    levels, rows, width = adj_u.shape
    bands, segments = lax.axis_size("lat"), lax.axis_size("lon")
    band = lax.axis_index("lat")
    total_rows = rows * bands
    tall = 2 * rows + PAD_ROWS
    matrices, twist, weight = filter_tables(segments, width)
    params = pltpu.CompilerParams(vmem_limit_bytes=VMEM_LIMIT)
    large = pltpu.CompilerParams(vmem_limit_bytes=VMEM_LARGE)
    in_vmem = pl.BlockSpec(memory_space=pltpu.VMEM)

    north_to_south = [(i + 1, i) for i in range(bands - 1)]
    south_to_north = [(i, i + 1) for i in range(bands - 1)]
    east_to_west = [((i + 1) % segments, i) for i in range(segments)]

    block = lambda at: pl.BlockSpec((levels, PAD_ROWS, width), lambda i, at=at: (0, at, 0))
    first, last = block(0), block(rows // PAD_ROWS - 1)
    to_south, to_north = pl.pallas_call(
        edge_kernel,
        grid=(1,),
        in_specs=[first, first, last],
        out_specs=[
            pl.BlockSpec((2, levels, width), lambda i: (0, 0, 0)),
            pl.BlockSpec((levels, width), lambda i: (0, 0)),
        ],
        out_shape=[
            jax.ShapeDtypeStruct((2, levels, width), jnp.float32),
            jax.ShapeDtypeStruct((levels, width), jnp.float32),
        ],
        compiler_params=large,
    )(adj_u, adj_v, adj_v)
    from_north = lax.ppermute(to_south, "lat", north_to_south)
    from_south = lax.ppermute(to_north, "lat", south_to_north)
    step = 8
    field = pl.BlockSpec((step, rows, width), lambda i: (i, 0, 0))
    pair = pl.pallas_call(
        pair_kernel,
        grid=(levels // step,),
        in_specs=[
            field,
            field,
            pl.BlockSpec((step, width), lambda i: (i, 0)),
            pl.BlockSpec((2, step, width), lambda i: (0, i, 0)),
        ],
        out_specs=pl.BlockSpec((step, tall, width), lambda i: (i, 0, 0)),
        out_shape=jax.ShapeDtypeStruct((levels, tall, width), jnp.float32),
        compiler_params=large,
    )(adj_u, adj_v, from_south, from_north)
    circles = swap(pair)

    def edge_sum(pick):
        theta, depth = pick(theta_traj), pick(dp_traj)
        return pick(adj_thick) + KAPPA * (theta / depth) * pick(adj_theta), theta, depth

    north = jnp.stack(edge_sum(lambda x: x[:, 0, :]))
    north = lax.ppermute(north, "lat", north_to_south)
    east = jnp.stack(edge_sum(lambda x: x[:, :, 0]))
    east = jnp.pad(east, ((0, 0), (0, 0), (0, LANES - rows)))
    east = lax.ppermute(east, "lon", east_to_west)

    whole = pl.BlockSpec(memory_space=pltpu.SMEM)
    spread_rows = jax.ShapeDtypeStruct((tall, LANES), jnp.float32)
    limit, flag = pl.pallas_call(
        rows_kernel,
        in_specs=[whole, whole, in_vmem, in_vmem],
        out_specs=[in_vmem, in_vmem],
        out_shape=[spread_rows, spread_rows],
        compiler_params=params,
    )(cutoff, polar_flags, cutoff.reshape(-1, LANES), polar_flags.reshape(-1, LANES))
    face, metric = row_geometry(band * rows + jnp.arange(rows + PAD_ROWS, dtype=jnp.int32), total_rows)
    geo = jnp.stack([spread(metric), spread(face)])

    half = segments // 2
    depth_of_work = ceil_to((half - 1) * tall, 16) + ceil_to(tall, 16)
    smooth = pl.pallas_call(
        filter_kernel,
        out_shape=jax.ShapeDtypeStruct((segments, tall, width), jnp.float32),
        scratch_shapes=[
            pltpu.VMEM((depth_of_work, 2 * width), jnp.float32),
        ],
        compiler_params=params,
    )(circles, limit, flag, geo, twist, weight, *matrices)
    winds = swap(smooth)

    step = 4
    field = pl.BlockSpec((step, rows, width), lambda i: (i, 0, 0))
    lines = pl.BlockSpec((3, None, step, width), lambda i: (0, i, 0, 0))
    grouped = lambda x: x[:3].reshape(3, levels // step, step, width)
    return pl.pallas_call(
        substep_kernel,
        grid=(levels // step,),
        in_specs=[
            pl.BlockSpec((step, tall, width), lambda i: (i, 0, 0)),
            field,
            field,
            field,
            field,
            pl.BlockSpec((2, rows + PAD_ROWS, width), lambda i: (0, 0, 0)),
            lines,
            lines,
        ],
        out_specs=[field] * 4,
        out_shape=[jax.ShapeDtypeStruct(adj_u.shape, jnp.float32)] * 4,
        compiler_params=params,
    )(winds, adj_thick, adj_theta, theta_traj, dp_traj, geo, grouped(north), grouped(east))


def solution(mesh):
    field = P(None, "lat", "lon")
    return jax.shard_map(
        shards,
        mesh=mesh,
        in_specs=(field,) * 6 + (P(), P()),
        out_specs=(field,) * 4,
        check_vma=False,
    )
```

time: 152 us -> 99.6 us (0.66)
  the two profiles are of different devices: /device:TPU:1 before, /device:TPU:64 now
where the time goes in v1:
time: 99.6 us; the launch traced here: 99.1 us
  waiting for transfers between devices  57 us (57%)
  starting transfers between devices  26.9 us (27%)
  Pallas kernels  11.8 us (12%)
  local copies, waits for them, and re-layouts  2.33 us (2%)
    all_to_all x2, waiting for transfers between devices, swap(): lax.all_to_all(blocks, 'lon', split_axis=0, concat_axis=0, tiled=True)  36.5 us
    ppermute x1, waiting for transfers between devices, shards(): north = lax.ppermute(north, 'lat', north_to_south)  14.2 us
    all_to_all x2, starting transfers between devices, swap(): lax.all_to_all(blocks, 'lon', split_axis=0, concat_axis=0, tiled=True)  12.6 us
    ppermute x1, starting transfers between devices, shards(): east = lax.ppermute(east, 'lon', east_to_west)  8.05 us
    ppermute x1, waiting for transfers between devices, shards(): from_south = lax.ppermute(to_north, 'lat', south_to_north)  6.16 us
    pallas_call x1, Pallas kernels, shards(): pl.pallas_call(filter_kernel, out_shape=jax.ShapeDtypeStruct((segments, t...  4.12 us
    pallas_call x1, Pallas kernels, shards(): pl.pallas_call(substep_kernel, grid=(levels // step,), in_specs=[pl.Block...  3.16 us
    ppermute x1, starting transfers between devices, shards(): from_south = lax.ppermute(to_north, 'lat', south_to_north)  2.41 us
  transfers between devices with their start and end apart: 6, of which 5 were waited for; matrix products, arithmetic and copies ran while one was open for 1% of the time, Pallas kernels for 1%

profile of v1, /device:TPU:64, one launch (start us, length us, event | category | flops | bytes accessed | tf_op | source)
XLA Modules:
  0.0 99.1 jit_solution(2391201626595009778)
XLA Ops:
  0.6 1.5 %shard_map.201 = (f32[2,16,128]{2,1,0:T(8,128)}, f32[16,128]{1,0:T(8,128)}) custom-call(f32[16,64,128]{2,1,0:T(8,128)} %u_ref.1, f32[16,64,128]{2,1,0:T(8,128)} %v_ref.1, f32[16,64,128]{2,1,0:T(8,128)} %v_ref.1), custom_call_target="tpu_custom_call" | custom-call | tf_op jit(solution)/shard_map/pallas_call | solution.py:332
  2.2 1.9 %collective-permute-start.1 = (f32[2,16,128]{2,1,0:T(8,128)}, f32[2,16,128]{2,1,0:T(8,128)S(1)}, u32[]{:S(2)}, u32[]{:S(2)}) collective-permute-start(f32[2,16,128]{2,1,0:T(8,128)} %get-tuple-element.9), channel_id=1, source_target_pairs={{16,0},{32,16},{48,32},{64,48},{80,64},{96,80},{112,96},{128,112},... | collective-permute-start | bytes 49160 | tf_op jit(solution)/shard_map/ppermute | solution.py:346
  4.1 2.4 %collective-permute-start = (f32[16,128]{1,0:T(8,128)}, f32[16,128]{1,0:T(8,128)S(1)}, u32[]{:S(2)}, u32[]{:S(2)}) collective-permute-start(f32[16,128]{1,0:T(8,128)} %get-tuple-element.8), channel_id=1, source_target_pairs={{0,16},{16,32},{32,48},{48,64},{64,80},{80,96},{96,112},{112,128},... | collective-permute-start | bytes 24584 | tf_op jit(solution)/shard_map/ppermute | solution.py:347
  6.5 6.2 %collective-permute-done.south_ref = f32[16,128]{1,0:T(8,128)S(1)} collective-permute-done((f32[16,128]{1,0:T(8,128)}, f32[16,128]{1,0:T(8,128)S(1)}, u32[]{:S(2)}, u32[]{:S(2)}) %collective-permute-start) | collective-permute-done | bytes 8224 | tf_op jit(solution)/shard_map/ppermute | solution.py:347
  12.7 0.6 copy-done.17
  13.3 0.6 copy-done.16
  13.9 2.1 %shard_map.202 = f32[16,136,128]{2,1,0:T(8,128)} custom-call(f32[16,64,128]{2,1,0:T(8,128)} %u_ref.1, f32[16,64,128]{2,1,0:T(8,128)} %v_ref.1, f32[16,128]{1,0:T(8,128)} %copy-done.17, f32[2,16,128]{2,1,0:T(8,128)} %copy-done.16), custom_call_target="tpu_custom_call" | custom-call | tf_op jit(solution)/shard_map/pallas_call | solution.py:350
  16.1 8.7 %all-to-all-start = ((f32[16,136,128]{2,1,0:T(8,128)}), f32[16,136,128]{2,1,0:T(8,128)S(1)}, u32[]{:S(2)}, u32[]{:S(2)}) async-start(f32[16,136,128]{2,1,0:T(8,128)} %shard_map.202), calls=%async_computation | async-start | bytes 2228224 | tf_op jit(solution)/shard_map/all_to_all | solution.py:312
  24.8 0.9 shard_map.203
  25.8 0.1 stack_broadcast_in_dim.5
  25.9 0.1 stack_broadcast_in_dim.4
  26.0 30.9 %all-to-all-done.x_ref = f32[16,136,128]{2,1,0:T(8,128)S(1)} async-done(((f32[16,136,128]{2,1,0:T(8,128)}), f32[16,136,128]{2,1,0:T(8,128)S(1)}, u32[]{:S(2)}, u32[]{:S(2)}) %all-to-all-start) | async-done | bytes 1114144 | tf_op jit(solution)/shard_map/all_to_all | solution.py:312
  57.0 4.1 %shard_map.204 = f32[16,136,128]{2,1,0:T(8,128)} custom-call(f32[16,136,128]{2,1,0:T(8,128)S(1)} %all-to-all-done.x_ref, f32[136,128]{1,0:T(8,128)S(1)} %get-tuple-element.10.limit_ref, f32[136,128]{1,0:T(8,128)S(1)} %get-tuple-element.11.flag_ref, f32[2,72,128]{2,1,0:T(8,128)S(1)} %pad_maximum_fusion.geo_ref, f32[2,7,128]{2,1,0:T(8,128)S(1)} %copy-done.15, ...), custom_call_target="tpu_custom_call" | custom-call | tf_op jit(solution)/shard_map/pallas_call | solution.py:389
  61.1 3.9 %all-to-all-start.1 = ((f32[16,136,128]{2,1,0:T(8,128)}), f32[16,136,128]{2,1,0:T(8,128)S(1)}, u32[]{:S(2)}, u32[]{:S(2)}) async-start(f32[16,136,128]{2,1,0:T(8,128)} %shard_map.204), calls=%async_computation.1 | async-start | bytes 2228224 | tf_op jit(solution)/shard_map/all_to_all | solution.py:312
  65.1 1.9 %collective-permute-start.2 = (f32[3,16,128]{2,1,0:T(8,128)S(1)}, f32[3,16,128]{2,1,0:T(8,128)S(1)}, u32[]{:S(2)}, u32[]{:S(2)}) collective-permute-start(f32[3,16,128]{2,1,0:T(8,128)S(1)} %pad_maximum_fusion.1), channel_id=1, source_target_pairs={{16,0},{32,16},{48,32},{64,48},{80,64},{96,80},{112,96},{128,112},... | collective-permute-start | bytes 73736 | tf_op jit(solution)/shard_map/ppermute | solution.py:370
  67.0 0.2 copy.40
  67.3 0.2 copy.39
  67.5 0.2 copy.38
  67.7 0.2 copy.41
  68.0 8.1 %collective-permute-start.3 = (f32[3,16,128]{2,1,0:T(8,128)S(1)}, f32[3,16,128]{2,1,0:T(8,128)S(1)}, u32[]{:S(2)}, u32[]{:S(2)}) collective-permute-start(f32[3,16,128]{2,1,0:T(8,128)S(1)} %select_maximum_fusion), channel_id=1, source_target_pairs={{1,0},{2,1},{3,2},{4,3},{5,4},{6,5},{7,6},{8,7},{9,8},{10,9},{11,1... | collective-permute-start | bytes 73736 | tf_op jit(solution)/shard_map/ppermute | solution.py:373
  76.0 14.2 %collective-permute-done.2 = f32[3,16,128]{2,1,0:T(8,128)S(1)} collective-permute-done((f32[3,16,128]{2,1,0:T(8,128)S(1)}, f32[3,16,128]{2,1,0:T(8,128)S(1)}, u32[]{:S(2)}, u32[]{:S(2)}) %collective-permute-start.2) | collective-permute-done | bytes 24608 | tf_op jit(solution)/shard_map/ppermute | solution.py:370
  90.2 0.2 collective-permute-done.3
  90.4 5.5 %all-to-all-done.1.winds_ref = f32[16,136,128]{2,1,0:T(8,128)S(1)} async-done(((f32[16,136,128]{2,1,0:T(8,128)}), f32[16,136,128]{2,1,0:T(8,128)S(1)}, u32[]{:S(2)}, u32[]{:S(2)}) %all-to-all-start.1) | async-done | bytes 1114144 | tf_op jit(solution)/shard_map/all_to_all | solution.py:312
  96.0 3.2 %shard_map.205 = (f32[16,64,128]{2,1,0:T(8,128)}, f32[16,64,128]{2,1,0:T(8,128)}, f32[16,64,128]{2,1,0:T(8,128)}, f32[16,64,128]{2,1,0:T(8,128)}) custom-call(f32[16,136,128]{2,1,0:T(8,128)S(1)} %all-to-all-done.1.winds_ref, f32[16,64,128]{2,1,0:T(8,128)S(1)} %copy-done, f32[16,64,128]{2,1,0:T(8,128)S(1)} %copy-done.1, f32[16,64,128]{2,1,0:T(8,128)S(1)} %copy-done.2, ...), custom_call_target="tpu_custom_call" | custom-call | tf_op jit(solution)/shard_map/pallas_call | solution.py:403
  (45 shorter events, 0.3 us)
Async XLA Ops:
  2.2 10.5 %collective-permute-start.1 = (f32[2,16,128]{2,1,0:T(8,128)}, f32[2,16,128]{2,1,0:T(8,128)S(1)}, u32[]{:S(2)}, u32[]{:S(2)}) collective-permute-start(f32[2,16,128]{2,1,0:T(8,128)} %get-tuple-element.9), channel_id=1, source_target_pairs={{16,0},{32,16},{48,32},{64,48},{80,64},{96,80},{112,96},{128,112},... | collective-permute-start | bytes 49160 | tf_op jit(solution)/shard_map/ppermute | solution.py:346
  4.1 8.6 %collective-permute-start = (f32[16,128]{1,0:T(8,128)}, f32[16,128]{1,0:T(8,128)S(1)}, u32[]{:S(2)}, u32[]{:S(2)}) collective-permute-start(f32[16,128]{1,0:T(8,128)} %get-tuple-element.8), channel_id=1, source_target_pairs={{0,16},{16,32},{32,48},{48,64},{64,80},{80,96},{96,112},{112,128},... | collective-permute-start | bytes 24584 | tf_op jit(solution)/shard_map/ppermute | solution.py:347
  12.7 0.6 copy-start.17
  13.3 0.6 copy-start.16
  15.9 8.9 %copy-start.12 = (s32[2048]{0:T(1024)S(1)}, s32[2048]{0:T(1024)}, u32[]{:S(2)}) copy-start(s32[2048]{0:T(1024)} %limits_ref.1) | copy-start | bytes 24580
  16.0 8.9 %copy-start.13 = (s32[2048]{0:T(1024)S(1)}, s32[2048]{0:T(1024)}, u32[]{:S(2)}) copy-start(s32[2048]{0:T(1024)} %flags_ref.1) | copy-start | bytes 24580
  16.0 40.9 %copy-start.4 = (bf16[256,256]{1,0:T(8,128)(2,1)S(1)}, bf16[256,256]{1,0:T(8,128)(2,1)}, u32[]{:S(2)}) copy-start(bf16[256,256]{1,0:T(8,128)(2,1)} %constant.56.clone.rest_7_) | copy-start | bytes 393220
  16.0 40.9 %copy-start.5 = (bf16[256,256]{1,0:T(8,128)(2,1)S(1)}, bf16[256,256]{1,0:T(8,128)(2,1)}, u32[]{:S(2)}) copy-start(bf16[256,256]{1,0:T(8,128)(2,1)} %constant.55.clone.rest_6_) | copy-start | bytes 393220
  16.0 40.9 %copy-start.6 = (bf16[256,256]{1,0:T(8,128)(2,1)S(1)}, bf16[256,256]{1,0:T(8,128)(2,1)}, u32[]{:S(2)}) copy-start(bf16[256,256]{1,0:T(8,128)(2,1)} %constant.54.clone.rest_5_) | copy-start | bytes 393220
  16.0 40.9 %copy-start.7 = (bf16[256,256]{1,0:T(8,128)(2,1)S(1)}, bf16[256,256]{1,0:T(8,128)(2,1)}, u32[]{:S(2)}) copy-start(bf16[256,256]{1,0:T(8,128)(2,1)} %constant.53.clone.rest_4_) | copy-start | bytes 393220
  16.0 40.9 %copy-start.8 = (bf16[256,256]{1,0:T(8,128)(2,1)S(1)}, bf16[256,256]{1,0:T(8,128)(2,1)}, u32[]{:S(2)}) copy-start(bf16[256,256]{1,0:T(8,128)(2,1)} %constant.52.clone.rest_3_) | copy-start | bytes 393220
  16.0 40.9 %copy-start.9 = (bf16[256,256]{1,0:T(8,128)(2,1)S(1)}, bf16[256,256]{1,0:T(8,128)(2,1)}, u32[]{:S(2)}) copy-start(bf16[256,256]{1,0:T(8,128)(2,1)} %constant.51.clone.rest_2_) | copy-start | bytes 393220
  16.0 40.9 %copy-start.10 = (bf16[256,256]{1,0:T(8,128)(2,1)S(1)}, bf16[256,256]{1,0:T(8,128)(2,1)}, u32[]{:S(2)}) copy-start(bf16[256,256]{1,0:T(8,128)(2,1)} %constant.50.clone.rest_1_) | copy-start | bytes 393220
  16.0 40.9 %copy-start.11 = (bf16[256,256]{1,0:T(8,128)(2,1)S(1)}, bf16[256,256]{1,0:T(8,128)(2,1)}, u32[]{:S(2)}) copy-start(bf16[256,256]{1,0:T(8,128)(2,1)} %constant.49.clone.rest_0_) | copy-start | bytes 393220
  16.1 40.9 %copy-start.14 = (f32[2,8,256]{2,1,0:T(8,128)S(1)}, f32[2,8,256]{2,1,0:T(8,128)}, u32[]{:S(2)}) copy-start(f32[2,8,256]{2,1,0:T(8,128)} %constant.58.clone.weight_ref) | copy-start | bytes 49156
  16.1 40.9 %copy-start.15 = (f32[2,7,128]{2,1,0:T(8,128)S(1)}, f32[2,7,128]{2,1,0:T(8,128)}, u32[]{:S(2)}) copy-start(f32[2,7,128]{2,1,0:T(8,128)} %constant.57.clone.twist_ref) | copy-start | bytes 21508
  16.1 40.8 %all-to-all-start = ((f32[16,136,128]{2,1,0:T(8,128)}), f32[16,136,128]{2,1,0:T(8,128)S(1)}, u32[]{:S(2)}, u32[]{:S(2)}) async-start(f32[16,136,128]{2,1,0:T(8,128)} %shard_map.202), calls=%async_computation | async-start | bytes 2228224 | tf_op jit(solution)/shard_map/all_to_all | solution.py:312
  61.1 3.9 %copy-start.2 = (f32[16,64,128]{2,1,0:T(8,128)S(1)}, f32[16,64,128]{2,1,0:T(8,128)}, u32[]{:S(2)}) copy-start(f32[16,64,128]{2,1,0:T(8,128)} %traj_ref.1) | copy-start | bytes 1572868
  61.1 3.9 %copy-start.3 = (f32[16,64,128]{2,1,0:T(8,128)S(1)}, f32[16,64,128]{2,1,0:T(8,128)}, u32[]{:S(2)}) copy-start(f32[16,64,128]{2,1,0:T(8,128)} %depth_ref.1) | copy-start | bytes 1572868
  61.1 3.9 %copy-start.1 = (f32[16,64,128]{2,1,0:T(8,128)S(1)}, f32[16,64,128]{2,1,0:T(8,128)}, u32[]{:S(2)}) copy-start(f32[16,64,128]{2,1,0:T(8,128)} %theta_ref.1) | copy-start | bytes 1572868
  61.1 4.0 %copy-start = (f32[16,64,128]{2,1,0:T(8,128)S(1)}, f32[16,64,128]{2,1,0:T(8,128)}, u32[]{:S(2)}) copy-start(f32[16,64,128]{2,1,0:T(8,128)} %thick_ref.1) | copy-start | bytes 1572868
  61.1 34.8 %all-to-all-start.1 = ((f32[16,136,128]{2,1,0:T(8,128)}), f32[16,136,128]{2,1,0:T(8,128)S(1)}, u32[]{:S(2)}, u32[]{:S(2)}) async-start(f32[16,136,128]{2,1,0:T(8,128)} %shard_map.204), calls=%async_computation.1 | async-start | bytes 2228224 | tf_op jit(solution)/shard_map/all_to_all | solution.py:312
  65.1 25.1 %collective-permute-start.2 = (f32[3,16,128]{2,1,0:T(8,128)S(1)}, f32[3,16,128]{2,1,0:T(8,128)S(1)}, u32[]{:S(2)}, u32[]{:S(2)}) collective-permute-start(f32[3,16,128]{2,1,0:T(8,128)S(1)} %pad_maximum_fusion.1), channel_id=1, source_target_pairs={{16,0},{32,16},{48,32},{64,48},{80,64},{96,80},{112,96},{128,112},... | collective-permute-start | bytes 73736 | tf_op jit(solution)/shard_map/ppermute | solution.py:370
  68.0 22.5 %collective-permute-start.3 = (f32[3,16,128]{2,1,0:T(8,128)S(1)}, f32[3,16,128]{2,1,0:T(8,128)S(1)}, u32[]{:S(2)}, u32[]{:S(2)}) collective-permute-start(f32[3,16,128]{2,1,0:T(8,128)S(1)} %select_maximum_fusion), channel_id=1, source_target_pairs={{1,0},{2,1},{3,2},{4,3},{5,4},{6,5},{7,6},{8,7},{9,8},{10,9},{11,1... | collective-permute-start | bytes 73736 | tf_op jit(solution)/shard_map/ppermute | solution.py:373

commit v2 on v1

--- a/solution.py
+++ b/solution.py
@@ -133,7 +133,7 @@
             work_ref[to, :width] = re * cos + im * sin
             work_ref[to, width:] = im * cos - re * sin
 
-    limit = limit_ref[...]
+    limit = limit_ref[:rows, :]
     limit = limit * limit
     limit = jnp.concatenate([limit, limit], axis=1)
 
@@ -170,85 +170,95 @@
     return lax.broadcasted_iota(jnp.int32, shape, len(shape) - 1)
 
 
-def gather_columns(out_ref, start, rows, picks):
+def gather_columns(out_ref, rows, picks):
     shape = (rows, LANES)
     lanes = lane_index(shape)
     total = jnp.zeros(shape, jnp.float32)
     for q, a, lane in picks:
-        column = jnp.broadcast_to(out_ref[a, start : start + rows, lane : lane + 1], shape)
+        column = jnp.broadcast_to(out_ref[a, :rows, lane : lane + 1], shape)
         total = jnp.where(lanes == q, column, total)
     return total
 
 
-def edge_kernel(u_first_ref, v_first_ref, v_last_ref, north_ref, south_ref):
-    north_ref[0] = u_first_ref[:, 0, :]
-    north_ref[1] = v_first_ref[:, 0, :]
+def edge_kernel(u_ref, v_first_ref, v_last_ref, thick_ref, theta_ref, traj_ref, depth_ref, north_ref, south_ref):
+    traj, depth = traj_ref[:, 0, :], depth_ref[:, 0, :]
+    north_ref[0] = thick_ref[:, 0, :] + KAPPA * (traj / depth) * theta_ref[:, 0, :]
+    north_ref[1] = traj
+    north_ref[2] = depth
+    north_ref[3] = u_ref[:, 0, :]
+    north_ref[4] = v_first_ref[:, 0, :]
     south_ref[...] = v_last_ref[:, PAD_ROWS - 1, :]
 
 
-def pair_kernel(u_ref, v_ref, south_ref, north_ref, out_ref):
-    levels, rows, width = u_ref.shape
-    main = 2 * rows
-    out_ref[:, :rows, :] = u_ref[...]
-    out_ref[:, rows:main, :] = v_ref[...]
-    out_ref[:, main:, :] = jnp.zeros((levels, PAD_ROWS, width), jnp.float32)
-    out_ref[:, main, :] = south_ref[...]
-    out_ref[:, main + 1, :] = north_ref[1]
-    out_ref[:, main + 2, :] = north_ref[0]
-
-
-def rows_kernel(limits_ref, flags_ref, limit_block_ref, flag_block_ref, limit_out, flag_out):
-    rows = (limit_out.shape[0] - PAD_ROWS) // 2
+def pair_kernel(v_ref, south_ref, north_ref, out_ref):
+    rows = v_ref.shape[1]
+    out_ref[:, :rows, :] = v_ref[...]
+    out_ref[:, rows:, :] = jnp.zeros(out_ref[:, rows:, :].shape, jnp.float32)
+    out_ref[:, rows, :] = south_ref[...]
+    out_ref[:, rows + 1, :] = north_ref[4]
+    out_ref[:, rows + 2, :] = north_ref[3]
+
+
+def rows_kernel(limits_ref, flags_ref, limit_block_ref, flag_block_ref, limit_out, flag_out, line_ref):
+    rows = limit_out.shape[0] - PAD_ROWS
     count = limits_ref.shape[0]
     first = lax.axis_index("lat") * rows
-    block, part = first // LANES, (first % LANES) // rows
     south, north = jnp.maximum(first - 1, 0), jnp.minimum(first + rows, count - 1)
     sub = lax.broadcasted_iota(jnp.int32, (PAD_ROWS, LANES), 0)
-    for line_ref, scalar_ref, out_ref in (
+    for block_ref, scalar_ref, out_ref in (
         (limit_block_ref, limits_ref, limit_out),
         (flag_block_ref, flags_ref, flag_out),
     ):
-        line = jnp.broadcast_to(line_ref[pl.ds(block, 1), :].astype(jnp.float32), (LANES, LANES)).T
-        own = line[:rows]
-        for p in range(1, LANES // rows):
-            own = jnp.where(part == p, line[p * rows : (p + 1) * rows], own)
-        out_ref[:rows, :] = own
-        out_ref[rows : 2 * rows, :] = own
+        line = block_ref[pl.ds(first // LANES, 1), :].astype(jnp.float32)
+        line_ref[...] = jnp.broadcast_to(line, (LANES, LANES)).T
+        out_ref[:rows, :] = line_ref[pl.ds(pl.multiple_of(first % LANES, rows), rows), :]
         tail = jnp.where(sub == 0, scalar_ref[south], scalar_ref[north])
-        out_ref[2 * rows :, :] = tail.astype(jnp.float32)
-
-
-def filter_kernel(x_ref, limit_ref, flag_ref, geo_ref, twist_ref, weight_ref, *rest):
-    matrices, (out_ref, work_ref) = rest[:8], rest[8:]
-    segments, tall, width = x_ref.shape
-    main = tall - PAD_ROWS
-    rows = main // 2
-    metric = geo_ref[0, :rows, :]
-    metric_north = geo_ref[0, rows : rows + 1, :]
-    edge = lane_index((1, width)) == 0
-    filter_body(x_ref, limit_ref, flag_ref, twist_ref, weight_ref, matrices, out_ref, work_ref)
-    u_north = [out_ref[a, main + 2 : main + 3, :] for a in range(segments)]
-    rolled = [pltpu.roll(u_north[a], 1, 1) for a in range(segments)]
+        out_ref[rows:, :] = tail.astype(jnp.float32)
+
+
+def filter_u_kernel(x_ref, limit_ref, flag_ref, twist_ref, weight_ref, *rest):
+    matrices, (out_ref, side_ref, smooth_ref, work_ref, sem) = rest[:8], rest[8:]
+    segments, rows, width = x_ref.shape
+    filter_body(x_ref, limit_ref, flag_ref, twist_ref, weight_ref, matrices, smooth_ref, work_ref)
+    copy = pltpu.make_async_copy(smooth_ref, out_ref.at[:, :rows, :], sem)
+    copy.start()
     last = width - 1
     ahead = [(a, (a + 1) % segments, 0) for a in range(segments)]
     behind = [(segments + a, (a - 1) % segments, last) for a in range(segments)]
     own = [(a, a, last) for a in range(segments)]
-    side = gather_columns(out_ref, 0, rows, ahead + behind) - gather_columns(out_ref, 0, rows, own)
-    v_ahead = gather_columns(out_ref, rows, rows + 1, ahead)
+    side_ref[...] = gather_columns(smooth_ref, rows, ahead + behind) - gather_columns(smooth_ref, rows, own)
+    copy.wait()
+
+
+def filter_v_kernel(x_ref, limit_ref, flag_ref, geo_ref, side_ref, twist_ref, weight_ref, *rest):
+    matrices, (_, out_ref, smooth_ref, work_ref, sem) = rest[:8], rest[8:]
+    segments, tall, width = x_ref.shape
+    rows = tall - PAD_ROWS
+    filter_body(x_ref, limit_ref, flag_ref, twist_ref, weight_ref, matrices, smooth_ref, work_ref)
+    metric = geo_ref[0, :rows, :]
+    metric_north = geo_ref[0, rows : rows + 1, :]
+    edge = lane_index((1, width)) == 0
+    u_north = [smooth_ref[a, rows + 2 : rows + 3, :] for a in range(segments)]
+    rolled = [pltpu.roll(u_north[a], 1, 1) for a in range(segments)]
+    ahead = [(a, (a + 1) % segments, 0) for a in range(segments)]
+    v_ahead = gather_columns(smooth_ref, rows + 1, ahead)
     v_body = v_ahead[:rows]
     top = lax.broadcasted_iota(jnp.int32, (rows, LANES), 0) == 0
     v_south = jnp.where(top, v_ahead[rows : rows + 1], pltpu.roll(v_body, 1, 0))
+    side = side_ref[...]
     mixed = CROSS * metric * side + MERID * (v_body - v_south)
     columns = jnp.where(lane_index((rows, LANES)) < segments, mixed, side)
     columns = jnp.concatenate([columns, jnp.zeros((LANES - rows, LANES), jnp.float32)], axis=0).T
     for a in range(segments):
         west = jnp.where(edge, rolled[a - 1], rolled[a])
-        north = CROSS * metric_north * (u_north[a] - west) + MERID * (
-            out_ref[a, main + 1 : main + 2, :] - out_ref[a, main - 1 : main, :]
+        smooth_ref[a, rows + 1 : rows + 2, :] = CROSS * metric_north * (u_north[a] - west) + MERID * (
+            smooth_ref[a, rows + 1 : rows + 2, :] - smooth_ref[a, rows - 1 : rows, :]
         )
-        out_ref[a, main + 1 : main + 2, :] = north
-        out_ref[a, main + 2 : main + 3, :] = columns[a : a + 1]
-        out_ref[a, main + 3 : main + 4, :] = columns[segments + a : segments + a + 1]
+        smooth_ref[a, rows + 2 : rows + 3, :] = columns[a : a + 1]
+        smooth_ref[a, rows + 3 : rows + 4, :] = columns[segments + a : segments + a + 1]
+    copy = pltpu.make_async_copy(smooth_ref, out_ref.at[:, rows:, :], sem)
+    copy.start()
+    copy.wait()
 
 
 def substep_kernel(
@@ -317,104 +327,115 @@
     bands, segments = lax.axis_size("lat"), lax.axis_size("lon")
     band = lax.axis_index("lat")
     total_rows = rows * bands
-    tall = 2 * rows + PAD_ROWS
+    tall, whole_block = rows + PAD_ROWS, 2 * rows + PAD_ROWS
     matrices, twist, weight = filter_tables(segments, width)
     params = pltpu.CompilerParams(vmem_limit_bytes=VMEM_LIMIT)
     large = pltpu.CompilerParams(vmem_limit_bytes=VMEM_LARGE)
     in_vmem = pl.BlockSpec(memory_space=pltpu.VMEM)
-
+    in_hbm = pl.BlockSpec(memory_space=pltpu.HBM)
+    in_smem = pl.BlockSpec(memory_space=pltpu.SMEM)
+    f32 = lambda *shape: jax.ShapeDtypeStruct(shape, jnp.float32)
     north_to_south = [(i + 1, i) for i in range(bands - 1)]
     south_to_north = [(i, i + 1) for i in range(bands - 1)]
     east_to_west = [((i + 1) % segments, i) for i in range(segments)]
+
+    circles_u = swap(adj_u)
 
     block = lambda at: pl.BlockSpec((levels, PAD_ROWS, width), lambda i, at=at: (0, at, 0))
     first, last = block(0), block(rows // PAD_ROWS - 1)
     to_south, to_north = pl.pallas_call(
         edge_kernel,
         grid=(1,),
-        in_specs=[first, first, last],
+        in_specs=[first, first, last, first, first, first, first],
         out_specs=[
-            pl.BlockSpec((2, levels, width), lambda i: (0, 0, 0)),
+            pl.BlockSpec((5, levels, width), lambda i: (0, 0, 0)),
             pl.BlockSpec((levels, width), lambda i: (0, 0)),
         ],
-        out_shape=[
-            jax.ShapeDtypeStruct((2, levels, width), jnp.float32),
-            jax.ShapeDtypeStruct((levels, width), jnp.float32),
-        ],
+        out_shape=[f32(5, levels, width), f32(levels, width)],
         compiler_params=large,
-    )(adj_u, adj_v, adj_v)
-    from_north = lax.ppermute(to_south, "lat", north_to_south)
-    from_south = lax.ppermute(to_north, "lat", south_to_north)
+    )(adj_u, adj_v, adj_v, adj_thick, adj_theta, theta_traj, dp_traj)
+    north = lax.ppermute(to_south, "lat", north_to_south)
+    south = lax.ppermute(to_north, "lat", south_to_north)
+    step = 8
+    circles_v = swap(
+        pl.pallas_call(
+            pair_kernel,
+            grid=(levels // step,),
+            in_specs=[
+                pl.BlockSpec((step, rows, width), lambda i: (i, 0, 0)),
+                pl.BlockSpec((step, width), lambda i: (i, 0)),
+                pl.BlockSpec((5, step, width), lambda i: (0, i, 0)),
+            ],
+            out_specs=pl.BlockSpec((step, tall, width), lambda i: (i, 0, 0)),
+            out_shape=f32(levels, tall, width),
+            compiler_params=large,
+        )(adj_v, south, north)
+    )
+
+    first_column = lambda x: x[:, :, 0]
+    traj, depth = first_column(theta_traj), first_column(dp_traj)
+    change = first_column(adj_thick) + KAPPA * (traj / depth) * first_column(adj_theta)
+    east = jnp.stack([change, traj, depth])
+    east = jnp.pad(east, ((0, 0), (0, 0), (0, LANES - rows)))
+    east = lax.ppermute(east, "lon", east_to_west)
+
+    limit, flag = pl.pallas_call(
+        rows_kernel,
+        in_specs=[in_smem, in_smem, in_vmem, in_vmem],
+        out_specs=[in_vmem] * 2,
+        out_shape=[f32(tall, LANES)] * 2,
+        scratch_shapes=[pltpu.VMEM((LANES, LANES), jnp.float32)],
+        compiler_params=params,
+    )(cutoff, polar_flags, cutoff.reshape(-1, LANES), polar_flags.reshape(-1, LANES))
+    face, metric = row_geometry(band * rows + jnp.arange(tall, dtype=jnp.int32), total_rows)
+    geo = jnp.stack([spread(metric), spread(face)])
+
+    def scratch(count):
+        depth_of_work = ceil_to((segments // 2 - 1) * count, 16) + ceil_to(count, 16)
+        return [
+            pltpu.VMEM((segments, count, width), jnp.float32),
+            pltpu.VMEM((depth_of_work, 2 * width), jnp.float32),
+            pltpu.SemaphoreType.DMA,
+        ]
+
+    smooth, side = pl.pallas_call(
+        filter_u_kernel,
+        in_specs=[in_vmem] * 13,
+        out_specs=[in_hbm, in_vmem],
+        out_shape=[f32(segments, whole_block, width), f32(rows, LANES)],
+        scratch_shapes=scratch(rows),
+        compiler_params=params,
+    )(circles_u, limit, flag, twist, weight, *matrices)
+    smooth = pl.pallas_call(
+        filter_v_kernel,
+        in_specs=[in_vmem] * 15 + [in_hbm],
+        out_specs=in_hbm,
+        out_shape=f32(segments, whole_block, width),
+        input_output_aliases={15: 0},
+        scratch_shapes=scratch(tall),
+        compiler_params=params,
+    )(circles_v, limit, flag, geo, side, twist, weight, *matrices, smooth)
+    winds = swap(smooth)
+
     step = 8
     field = pl.BlockSpec((step, rows, width), lambda i: (i, 0, 0))
-    pair = pl.pallas_call(
-        pair_kernel,
-        grid=(levels // step,),
-        in_specs=[
-            field,
-            field,
-            pl.BlockSpec((step, width), lambda i: (i, 0)),
-            pl.BlockSpec((2, step, width), lambda i: (0, i, 0)),
-        ],
-        out_specs=pl.BlockSpec((step, tall, width), lambda i: (i, 0, 0)),
-        out_shape=jax.ShapeDtypeStruct((levels, tall, width), jnp.float32),
-        compiler_params=large,
-    )(adj_u, adj_v, from_south, from_north)
-    circles = swap(pair)
-
-    def edge_sum(pick):
-        theta, depth = pick(theta_traj), pick(dp_traj)
-        return pick(adj_thick) + KAPPA * (theta / depth) * pick(adj_theta), theta, depth
-
-    north = jnp.stack(edge_sum(lambda x: x[:, 0, :]))
-    north = lax.ppermute(north, "lat", north_to_south)
-    east = jnp.stack(edge_sum(lambda x: x[:, :, 0]))
-    east = jnp.pad(east, ((0, 0), (0, 0), (0, LANES - rows)))
-    east = lax.ppermute(east, "lon", east_to_west)
-
-    whole = pl.BlockSpec(memory_space=pltpu.SMEM)
-    spread_rows = jax.ShapeDtypeStruct((tall, LANES), jnp.float32)
-    limit, flag = pl.pallas_call(
-        rows_kernel,
-        in_specs=[whole, whole, in_vmem, in_vmem],
-        out_specs=[in_vmem, in_vmem],
-        out_shape=[spread_rows, spread_rows],
-        compiler_params=params,
-    )(cutoff, polar_flags, cutoff.reshape(-1, LANES), polar_flags.reshape(-1, LANES))
-    face, metric = row_geometry(band * rows + jnp.arange(rows + PAD_ROWS, dtype=jnp.int32), total_rows)
-    geo = jnp.stack([spread(metric), spread(face)])
-
-    half = segments // 2
-    depth_of_work = ceil_to((half - 1) * tall, 16) + ceil_to(tall, 16)
-    smooth = pl.pallas_call(
-        filter_kernel,
-        out_shape=jax.ShapeDtypeStruct((segments, tall, width), jnp.float32),
-        scratch_shapes=[
-            pltpu.VMEM((depth_of_work, 2 * width), jnp.float32),
-        ],
-        compiler_params=params,
-    )(circles, limit, flag, geo, twist, weight, *matrices)
-    winds = swap(smooth)
-
-    step = 4
-    field = pl.BlockSpec((step, rows, width), lambda i: (i, 0, 0))
-    lines = pl.BlockSpec((3, None, step, width), lambda i: (0, i, 0, 0))
-    grouped = lambda x: x[:3].reshape(3, levels // step, step, width)
+    lines = lambda count: pl.BlockSpec((count, None, step, width), lambda i: (0, i, 0, 0))
+    grouped = lambda x: x.reshape(x.shape[0], levels // step, step, width)
     return pl.pallas_call(
         substep_kernel,
         grid=(levels // step,),
         in_specs=[
-            pl.BlockSpec((step, tall, width), lambda i: (i, 0, 0)),
+            pl.BlockSpec((step, whole_block, width), lambda i: (i, 0, 0)),
             field,
             field,
             field,
             field,
-            pl.BlockSpec((2, rows + PAD_ROWS, width), lambda i: (0, 0, 0)),
-            lines,
-            lines,
+            pl.BlockSpec((2, tall, width), lambda i: (0, 0, 0)),
+            lines(5),
+            lines(3),
         ],
         out_specs=[field] * 4,
-        out_shape=[jax.ShapeDtypeStruct(adj_u.shape, jnp.float32)] * 4,
+        out_shape=[f32(levels, rows, width)] * 4,
         compiler_params=params,
     )(winds, adj_thick, adj_theta, theta_traj, dp_traj, geo, grouped(north), grouped(east))
 

time: 99.6 us -> 94.9 us (0.953)
  the two profiles are of different devices: /device:TPU:64 before, /device:TPU:40 now
where the time goes in v2:
time: 94.9 us; the launch traced here: 94.4 us
  waiting for transfers between devices  42.8 us (45%)
  starting transfers between devices  35.7 us (38%)
  Pallas kernels  11.2 us (12%)
  local copies, waits for them, and re-layouts  3.66 us (4%)
  between operations  0.97 us (1%)
    all_to_all x3, waiting for transfers between devices, swap(): lax.all_to_all(blocks, 'lon', split_axis=0, concat_axis=0, tiled=True)  27.3 us
    all_to_all x3, starting transfers between devices, swap(): lax.all_to_all(blocks, 'lon', split_axis=0, concat_axis=0, tiled=True)  22.3 us
    ppermute x1, waiting for transfers between devices, shards(): east = lax.ppermute(east, 'lon', east_to_west)  11.2 us
    ppermute x1, starting transfers between devices, shards(): east = lax.ppermute(east, 'lon', east_to_west)  8.06 us
    ppermute x1, waiting for transfers between devices, shards(): south = lax.ppermute(to_north, 'lat', south_to_north)  4.2 us
    unnamed x44, local copies, waits for them, and re-layouts  3.52 us
    ppermute x1, starting transfers between devices, shards(): north = lax.ppermute(to_south, 'lat', north_to_south)  3.31 us
    pallas_call x1, Pallas kernels, shards(): pl.pallas_call(substep_kernel, grid=(levels // step,), in_specs=[pl.Block...  3.09 us
  transfers between devices with their start and end apart: 6, of which 5 were waited for; matrix products, arithmetic and copies ran while one was open for 1% of the time, Pallas kernels for 7%

profile of v2, /device:TPU:40, one launch (start us, length us, event | category | flops | bytes accessed | tf_op | source)
XLA Modules:
  0.0 94.4 jit_solution(3320681846713817831)
XLA Ops:
  0.6 12.9 %all-to-all-start.1 = ((f32[16,64,128]{2,1,0:T(8,128)}), f32[16,64,128]{2,1,0:T(8,128)S(1)}, u32[]{:S(2)}, u32[]{:S(2)}) async-start(f32[16,64,128]{2,1,0:T(8,128)} %u_ref.1), calls=%async_computation.1 | async-start | bytes 1048576 | tf_op jit(solution)/shard_map/all_to_all | solution.py:322
  13.5 1.7 %shard_map.201 = (f32[5,16,128]{2,1,0:T(8,128)}, f32[16,128]{1,0:T(8,128)}) custom-call(f32[16,64,128]{2,1,0:T(8,128)} %u_ref.1, f32[16,64,128]{2,1,0:T(8,128)} %v_ref.1, f32[16,64,128]{2,1,0:T(8,128)} %v_ref.1, f32[16,64,128]{2,1,0:T(8,128)} %thick_ref.3, f32[16,64,128]{2,1,0:T(8,128)} %theta_ref.3, f32[16,64,128]{2,1,0:T(8,128)} %traj_ref.3, ...), custom_call_target="tpu_custom_call" | custom-call | tf_op jit(solution)/shard_map/pallas_call | solution.py:346
  15.2 3.3 %collective-permute-start.1 = (f32[5,16,128]{2,1,0:T(8,128)}, f32[5,16,128]{2,1,0:T(8,128)S(1)}, u32[]{:S(2)}, u32[]{:S(2)}) collective-permute-start(f32[5,16,128]{2,1,0:T(8,128)} %get-tuple-element.11), channel_id=1, source_target_pairs={{16,0},{32,16},{48,32},{64,48},{80,64},{96,80},{112,96},{128,112},... | collective-permute-start | bytes 122888 | tf_op jit(solution)/shard_map/ppermute | solution.py:357
  18.7 2.1 %collective-permute-start = (f32[16,128]{1,0:T(8,128)}, f32[16,128]{1,0:T(8,128)S(1)}, u32[]{:S(2)}, u32[]{:S(2)}) collective-permute-start(f32[16,128]{1,0:T(8,128)} %get-tuple-element.10), channel_id=1, source_target_pairs={{0,16},{16,32},{32,48},{48,64},{64,80},{80,96},{96,112},{112,128},... | collective-permute-start | bytes 24584 | tf_op jit(solution)/shard_map/ppermute | solution.py:358
  20.8 4.2 %collective-permute-done.south_ref = f32[16,128]{1,0:T(8,128)S(1)} collective-permute-done((f32[16,128]{1,0:T(8,128)}, f32[16,128]{1,0:T(8,128)S(1)}, u32[]{:S(2)}, u32[]{:S(2)}) %collective-permute-start) | collective-permute-done | bytes 8224 | tf_op jit(solution)/shard_map/ppermute | solution.py:358
  25.0 0.6 copy-done.19
  25.6 0.6 copy-done.13
  26.2 1.8 %shard_map.202 = f32[16,72,128]{2,1,0:T(8,128)} custom-call(f32[16,64,128]{2,1,0:T(8,128)} %v_ref.1, f32[16,128]{1,0:T(8,128)} %copy-done.19, f32[5,16,128]{2,1,0:T(8,128)} %copy-done.13), custom_call_target="tpu_custom_call" | custom-call | tf_op jit(solution)/shard_map/pallas_call | solution.py:361
  28.0 4.5 %all-to-all-done.1.x_ref = f32[16,64,128]{2,1,0:T(8,128)S(1)} async-done(((f32[16,64,128]{2,1,0:T(8,128)}), f32[16,64,128]{2,1,0:T(8,128)S(1)}, u32[]{:S(2)}, u32[]{:S(2)}) %all-to-all-start.1) | async-done | bytes 524320 | tf_op jit(solution)/shard_map/all_to_all | solution.py:322
  32.5 4.9 %all-to-all-start = ((f32[16,72,128]{2,1,0:T(8,128)}), f32[16,72,128]{2,1,0:T(8,128)S(1)}, u32[]{:S(2)}, u32[]{:S(2)}) async-start(f32[16,72,128]{2,1,0:T(8,128)} %shard_map.202), calls=%async_computation | async-start | bytes 1179648 | tf_op jit(solution)/shard_map/all_to_all | solution.py:322
  37.4 0.9 shard_map.203
  38.7 1.8 %shard_map.204 = (f32[16,136,128]{2,1,0:T(8,128)S(1)}, f32[64,128]{1,0:T(8,128)S(1)}) custom-call(f32[16,64,128]{2,1,0:T(8,128)S(1)} %all-to-all-done.1.x_ref, f32[72,128]{1,0:T(8,128)S(1)} %get-tuple-element.12.limit_ref, f32[72,128]{1,0:T(8,128)S(1)} %get-tuple-element.13.flag_ref, f32[2,7,128]{2,1,0:T(8,128)S(1)} %copy-done.16, ...), custom_call_target="tpu_custom_call" | custom-call | tf_op jit(solution)/shard_map/pallas_call | solution.py:401
  40.4 15.8 %all-to-all-done.x_ref = f32[16,72,128]{2,1,0:T(8,128)S(1)} async-done(((f32[16,72,128]{2,1,0:T(8,128)}), f32[16,72,128]{2,1,0:T(8,128)S(1)}, u32[]{:S(2)}, u32[]{:S(2)}) %all-to-all-start) | async-done | bytes 589856 | tf_op jit(solution)/shard_map/all_to_all | solution.py:322
  56.3 1.8 %shard_map.205 = f32[16,136,128]{2,1,0:T(8,128)S(1)} custom-call(f32[16,72,128]{2,1,0:T(8,128)S(1)} %all-to-all-done.x_ref, f32[72,128]{1,0:T(8,128)S(1)} %get-tuple-element.12.limit_ref, f32[72,128]{1,0:T(8,128)S(1)} %get-tuple-element.13.flag_ref, f32[2,72,128]{2,1,0:T(8,128)S(1)} %pad_maximum_fusion.geo_ref, ...), custom_call_target="tpu_custom_call", output_to_operand_aliasing={{}: (15, {})} | custom-call | tf_op jit(solution)/shard_map/pallas_call | solution.py:409
  58.1 1.0 %copy-done.4 = f32[16,136,128]{2,1,0:T(8,128)} copy-done((f32[16,136,128]{2,1,0:T(8,128)}, f32[16,136,128]{2,1,0:T(8,128)S(1)}, u32[]{:S(2)}) %copy-start.4) | copy-done | bytes 1114136
  59.1 4.6 %all-to-all-start.2 = ((f32[16,136,128]{2,1,0:T(8,128)}), f32[16,136,128]{2,1,0:T(8,128)S(1)}, u32[]{:S(2)}, u32[]{:S(2)}) async-start(f32[16,136,128]{2,1,0:T(8,128)} %copy-done.4), calls=%async_computation.2 | async-start | bytes 2228224 | tf_op jit(solution)/shard_map/all_to_all | solution.py:322
  63.7 0.2 copy.32
  63.9 0.2 copy.31
  64.2 0.2 copy.30
  64.4 0.4 copy-done.1
  65.0 8.1 %collective-permute-start.2 = (f32[3,16,128]{2,1,0:T(8,128)S(1)}, f32[3,16,128]{2,1,0:T(8,128)S(1)}, u32[]{:S(2)}, u32[]{:S(2)}) collective-permute-start(f32[3,16,128]{2,1,0:T(8,128)S(1)} %select_maximum_fusion), channel_id=1, source_target_pairs={{1,0},{2,1},{3,2},{4,3},{5,4},{6,5},{7,6},{8,7},{9,8},{10,9},{11,1... | collective-permute-start | bytes 73736 | tf_op jit(solution)/shard_map/ppermute | solution.py:380
  73.0 11.2 %collective-permute-done.2 = f32[3,16,128]{2,1,0:T(8,128)S(1)} collective-permute-done((f32[3,16,128]{2,1,0:T(8,128)S(1)}, f32[3,16,128]{2,1,0:T(8,128)S(1)}, u32[]{:S(2)}, u32[]{:S(2)}) %collective-permute-start.2) | collective-permute-done | bytes 24608 | tf_op jit(solution)/shard_map/ppermute | solution.py:380
  84.3 7.0 %all-to-all-done.2.winds_ref = f32[16,136,128]{2,1,0:T(8,128)S(1)} async-done(((f32[16,136,128]{2,1,0:T(8,128)}), f32[16,136,128]{2,1,0:T(8,128)S(1)}, u32[]{:S(2)}, u32[]{:S(2)}) %all-to-all-start.2) | async-done | bytes 1114144 | tf_op jit(solution)/shard_map/all_to_all | solution.py:322
  91.3 3.1 %shard_map.206 = (f32[16,64,128]{2,1,0:T(8,128)}, f32[16,64,128]{2,1,0:T(8,128)}, f32[16,64,128]{2,1,0:T(8,128)}, f32[16,64,128]{2,1,0:T(8,128)}) custom-call(f32[16,136,128]{2,1,0:T(8,128)S(1)} %all-to-all-done.2.winds_ref, f32[16,64,128]{2,1,0:T(8,128)S(1)} %copy-done, f32[16,64,128]{2,1,0:T(8,128)S(1)} %copy-done.1, f32[16,64,128]{2,1,0:T(8,128)S(1)} %copy-done.2, ...), custom_call_target="tpu_custom_call" | custom-call | tf_op jit(solution)/shard_map/pallas_call | solution.py:424
  (44 shorter events, 0.6 us)
Async XLA Ops:
  0.6 31.9 %all-to-all-start.1 = ((f32[16,64,128]{2,1,0:T(8,128)}), f32[16,64,128]{2,1,0:T(8,128)S(1)}, u32[]{:S(2)}, u32[]{:S(2)}) async-start(f32[16,64,128]{2,1,0:T(8,128)} %u_ref.1), calls=%async_computation.1 | async-start | bytes 1048576 | tf_op jit(solution)/shard_map/all_to_all | solution.py:322
  15.2 9.7 %collective-permute-start.1 = (f32[5,16,128]{2,1,0:T(8,128)}, f32[5,16,128]{2,1,0:T(8,128)S(1)}, u32[]{:S(2)}, u32[]{:S(2)}) collective-permute-start(f32[5,16,128]{2,1,0:T(8,128)} %get-tuple-element.11), channel_id=1, source_target_pairs={{16,0},{32,16},{48,32},{64,48},{80,64},{96,80},{112,96},{128,112},... | collective-permute-start | bytes 122888 | tf_op jit(solution)/shard_map/ppermute | solution.py:357
  18.5 18.9 %copy-start.17 = (s32[2048]{0:T(1024)S(1)}, s32[2048]{0:T(1024)}, u32[]{:S(2)}) copy-start(s32[2048]{0:T(1024)} %limits_ref.1) | copy-start | bytes 24580
  18.6 18.9 %copy-start.18 = (s32[2048]{0:T(1024)S(1)}, s32[2048]{0:T(1024)}, u32[]{:S(2)}) copy-start(s32[2048]{0:T(1024)} %flags_ref.1) | copy-start | bytes 24580
  18.6 20.0 %copy-start.5 = (bf16[256,256]{1,0:T(8,128)(2,1)S(1)}, bf16[256,256]{1,0:T(8,128)(2,1)}, u32[]{:S(2)}) copy-start(bf16[256,256]{1,0:T(8,128)(2,1)} %constant.55.clone.rest_7_) | copy-start | bytes 393220
  18.6 20.0 %copy-start.6 = (bf16[256,256]{1,0:T(8,128)(2,1)S(1)}, bf16[256,256]{1,0:T(8,128)(2,1)}, u32[]{:S(2)}) copy-start(bf16[256,256]{1,0:T(8,128)(2,1)} %constant.54.clone.rest_6_) | copy-start | bytes 393220
  18.6 20.0 %copy-start.7 = (bf16[256,256]{1,0:T(8,128)(2,1)S(1)}, bf16[256,256]{1,0:T(8,128)(2,1)}, u32[]{:S(2)}) copy-start(bf16[256,256]{1,0:T(8,128)(2,1)} %constant.53.clone.rest_5_) | copy-start | bytes 393220
  18.6 20.0 %copy-start.8 = (bf16[256,256]{1,0:T(8,128)(2,1)S(1)}, bf16[256,256]{1,0:T(8,128)(2,1)}, u32[]{:S(2)}) copy-start(bf16[256,256]{1,0:T(8,128)(2,1)} %constant.52.clone.rest_4_) | copy-start | bytes 393220
  18.6 20.0 %copy-start.9 = (bf16[256,256]{1,0:T(8,128)(2,1)S(1)}, bf16[256,256]{1,0:T(8,128)(2,1)}, u32[]{:S(2)}) copy-start(bf16[256,256]{1,0:T(8,128)(2,1)} %constant.51.clone.rest_3_) | copy-start | bytes 393220
  18.6 20.0 %copy-start.10 = (bf16[256,256]{1,0:T(8,128)(2,1)S(1)}, bf16[256,256]{1,0:T(8,128)(2,1)}, u32[]{:S(2)}) copy-start(bf16[256,256]{1,0:T(8,128)(2,1)} %constant.50.clone.rest_2_) | copy-start | bytes 393220
  18.6 20.0 %copy-start.11 = (bf16[256,256]{1,0:T(8,128)(2,1)S(1)}, bf16[256,256]{1,0:T(8,128)(2,1)}, u32[]{:S(2)}) copy-start(bf16[256,256]{1,0:T(8,128)(2,1)} %constant.49.clone.rest_1_) | copy-start | bytes 393220
  18.7 20.0 %copy-start.12 = (bf16[256,256]{1,0:T(8,128)(2,1)S(1)}, bf16[256,256]{1,0:T(8,128)(2,1)}, u32[]{:S(2)}) copy-start(bf16[256,256]{1,0:T(8,128)(2,1)} %constant.48.clone.rest_0_) | copy-start | bytes 393220
  18.7 20.0 %copy-start.15 = (f32[2,8,256]{2,1,0:T(8,128)S(1)}, f32[2,8,256]{2,1,0:T(8,128)}, u32[]{:S(2)}) copy-start(f32[2,8,256]{2,1,0:T(8,128)} %constant.57.clone.weight_ref) | copy-start | bytes 49156
  18.7 20.0 %copy-start.16 = (f32[2,7,128]{2,1,0:T(8,128)S(1)}, f32[2,7,128]{2,1,0:T(8,128)}, u32[]{:S(2)}) copy-start(f32[2,7,128]{2,1,0:T(8,128)} %constant.56.clone.twist_ref) | copy-start | bytes 21508
  18.7 6.3 %collective-permute-start = (f32[16,128]{1,0:T(8,128)}, f32[16,128]{1,0:T(8,128)S(1)}, u32[]{:S(2)}, u32[]{:S(2)}) collective-permute-start(f32[16,128]{1,0:T(8,128)} %get-tuple-element.10), channel_id=1, source_target_pairs={{0,16},{16,32},{32,48},{48,64},{64,80},{80,96},{96,112},{112,128},... | collective-permute-start | bytes 24584 | tf_op jit(solution)/shard_map/ppermute | solution.py:358
  32.5 23.7 %all-to-all-start = ((f32[16,72,128]{2,1,0:T(8,128)}), f32[16,72,128]{2,1,0:T(8,128)S(1)}, u32[]{:S(2)}, u32[]{:S(2)}) async-start(f32[16,72,128]{2,1,0:T(8,128)} %shard_map.202), calls=%async_computation | async-start | bytes 1179648 | tf_op jit(solution)/shard_map/all_to_all | solution.py:322
  58.1 1.0 %copy-start.4 = (f32[16,136,128]{2,1,0:T(8,128)}, f32[16,136,128]{2,1,0:T(8,128)S(1)}, u32[]{:S(2)}) copy-start(f32[16,136,128]{2,1,0:T(8,128)S(1)} %shard_map.205) | copy-start | bytes 3342340
  59.1 4.6 %copy-start.3 = (f32[16,64,128]{2,1,0:T(8,128)S(1)}, f32[16,64,128]{2,1,0:T(8,128)}, u32[]{:S(2)}) copy-start(f32[16,64,128]{2,1,0:T(8,128)} %depth_ref.3) | copy-start | bytes 1572868
  59.1 4.8 %copy-start.2 = (f32[16,64,128]{2,1,0:T(8,128)S(1)}, f32[16,64,128]{2,1,0:T(8,128)}, u32[]{:S(2)}) copy-start(f32[16,64,128]{2,1,0:T(8,128)} %traj_ref.3) | copy-start | bytes 1572868
  59.1 5.0 %copy-start = (f32[16,64,128]{2,1,0:T(8,128)S(1)}, f32[16,64,128]{2,1,0:T(8,128)}, u32[]{:S(2)}) copy-start(f32[16,64,128]{2,1,0:T(8,128)} %thick_ref.3) | copy-start | bytes 1572868
  59.1 32.2 %all-to-all-start.2 = ((f32[16,136,128]{2,1,0:T(8,128)}), f32[16,136,128]{2,1,0:T(8,128)S(1)}, u32[]{:S(2)}, u32[]{:S(2)}) async-start(f32[16,136,128]{2,1,0:T(8,128)} %copy-done.4), calls=%async_computation.2 | async-start | bytes 2228224 | tf_op jit(solution)/shard_map/all_to_all | solution.py:322
  63.7 1.0 %copy-start.1 = (f32[16,64,128]{2,1,0:T(8,128)S(1)}, f32[16,64,128]{2,1,0:T(8,128)}, u32[]{:S(2)}) copy-start(f32[16,64,128]{2,1,0:T(8,128)} %theta_ref.3) | copy-start | bytes 1572868
  63.7 27.6 %copy-start.14 = (f32[5,16,128]{2,1,0:T(8,128)S(1)}, f32[5,16,128]{2,1,0:T(8,128)}, u32[]{:S(2)}) copy-start(f32[5,16,128]{2,1,0:T(8,128)} %copy-done.13) | copy-start | bytes 122884
  65.0 19.3 %collective-permute-start.2 = (f32[3,16,128]{2,1,0:T(8,128)S(1)}, f32[3,16,128]{2,1,0:T(8,128)S(1)}, u32[]{:S(2)}, u32[]{:S(2)}) collective-permute-start(f32[3,16,128]{2,1,0:T(8,128)S(1)} %select_maximum_fusion), channel_id=1, source_target_pairs={{1,0},{2,1},{3,2},{4,3},{5,4},{6,5},{7,6},{8,7},{9,8},{10,9},{11,1... | collective-permute-start | bytes 73736 | tf_op jit(solution)/shard_map/ppermute | solution.py:380
  (2 other events, 1.2 us)

commit v3 on v2

--- a/solution.py
+++ b/solution.py
@@ -111,7 +111,7 @@
     return -(-value // step) * step
 
 
-def filter_body(x_ref, limit_ref, flag_ref, twist_ref, weight_ref, matrices, out_ref, work_ref):
+def filter_body(x_ref, limit_ref, flag_ref, twist_ref, weight_ref, matrices, out_ref, work_ref, emit=None):
     segments, rows, width = x_ref.shape
     half = segments // 2
     base = ceil_to((half - 1) * rows, 16)
@@ -149,9 +149,7 @@
     spectrum = split_product(work_ref[base : base + rows, :], real, real_low) * weights(0)
     work_ref[base : base + rows, :] = split_product(spectrum, real_back, real_back_low)
 
-    @pl.loop(0, rows // group)
-    def _(step):
-        at = pl.multiple_of(step * group, group)
+    def finish(at):
         here = pl.ds(at, group)
         first = pl.ds(pl.multiple_of(base + at, group), group)
         z = {}
@@ -164,6 +162,15 @@
         flagged = flag_ref[here, :] > 0.0
         for a in range(segments):
             out_ref[a, here, :] = jnp.where(flagged, smooth[a], x_ref[a, here, :])
+
+    @pl.loop(0, rows // group - 1)
+    def _(step):
+        at = pl.multiple_of(step * group, group)
+        finish(at)
+        if emit:
+            emit(step).start()
+
+    finish(rows - group)
 
 
 def lane_index(shape):
@@ -234,7 +241,13 @@
     matrices, (_, out_ref, smooth_ref, work_ref, sem) = rest[:8], rest[8:]
     segments, tall, width = x_ref.shape
     rows = tall - PAD_ROWS
-    filter_body(x_ref, limit_ref, flag_ref, twist_ref, weight_ref, matrices, smooth_ref, work_ref)
+
+    def emit(step):
+        at = pl.multiple_of(step * PAD_ROWS, PAD_ROWS)
+        source = smooth_ref.at[:, pl.ds(at, PAD_ROWS), :]
+        return pltpu.make_async_copy(source, out_ref.at[:, pl.ds(rows + at, PAD_ROWS), :], sem.at[step])
+
+    filter_body(x_ref, limit_ref, flag_ref, twist_ref, weight_ref, matrices, smooth_ref, work_ref, emit)
     metric = geo_ref[0, :rows, :]
     metric_north = geo_ref[0, rows : rows + 1, :]
     edge = lane_index((1, width)) == 0
@@ -256,9 +269,11 @@
         )
         smooth_ref[a, rows + 2 : rows + 3, :] = columns[a : a + 1]
         smooth_ref[a, rows + 3 : rows + 4, :] = columns[segments + a : segments + a + 1]
-    copy = pltpu.make_async_copy(smooth_ref, out_ref.at[:, rows:, :], sem)
-    copy.start()
-    copy.wait()
+    emit(rows // PAD_ROWS).start()
+
+    @pl.loop(0, tall // PAD_ROWS)
+    def _(step):
+        emit(step).wait()
 
 
 def substep_kernel(
@@ -334,6 +349,7 @@
     in_vmem = pl.BlockSpec(memory_space=pltpu.VMEM)
     in_hbm = pl.BlockSpec(memory_space=pltpu.HBM)
     in_smem = pl.BlockSpec(memory_space=pltpu.SMEM)
+    hbm = lambda *shape: pltpu.HBM(shape, jnp.float32)
     f32 = lambda *shape: jax.ShapeDtypeStruct(shape, jnp.float32)
     north_to_south = [(i + 1, i) for i in range(bands - 1)]
     south_to_north = [(i, i + 1) for i in range(bands - 1)]
@@ -367,8 +383,8 @@
                 pl.BlockSpec((5, step, width), lambda i: (0, i, 0)),
             ],
             out_specs=pl.BlockSpec((step, tall, width), lambda i: (i, 0, 0)),
-            out_shape=f32(levels, tall, width),
-            compiler_params=large,
+            out_shape=hbm(levels, tall, width),
+            compiler_params=params,
         )(adj_v, south, north)
     )
 
@@ -390,29 +406,29 @@
     face, metric = row_geometry(band * rows + jnp.arange(tall, dtype=jnp.int32), total_rows)
     geo = jnp.stack([spread(metric), spread(face)])
 
-    def scratch(count):
+    def scratch(count, copies):
         depth_of_work = ceil_to((segments // 2 - 1) * count, 16) + ceil_to(count, 16)
         return [
             pltpu.VMEM((segments, count, width), jnp.float32),
             pltpu.VMEM((depth_of_work, 2 * width), jnp.float32),
-            pltpu.SemaphoreType.DMA,
+            copies,
         ]
 
     smooth, side = pl.pallas_call(
         filter_u_kernel,
         in_specs=[in_vmem] * 13,
         out_specs=[in_hbm, in_vmem],
-        out_shape=[f32(segments, whole_block, width), f32(rows, LANES)],
-        scratch_shapes=scratch(rows),
+        out_shape=[hbm(segments, whole_block, width), f32(rows, LANES)],
+        scratch_shapes=scratch(rows, pltpu.SemaphoreType.DMA),
         compiler_params=params,
     )(circles_u, limit, flag, twist, weight, *matrices)
     smooth = pl.pallas_call(
         filter_v_kernel,
         in_specs=[in_vmem] * 15 + [in_hbm],
         out_specs=in_hbm,
-        out_shape=f32(segments, whole_block, width),
+        out_shape=hbm(segments, whole_block, width),
         input_output_aliases={15: 0},
-        scratch_shapes=scratch(tall),
+        scratch_shapes=scratch(tall, pltpu.SemaphoreType.DMA((tall // PAD_ROWS,))),
         compiler_params=params,
     )(circles_v, limit, flag, geo, side, twist, weight, *matrices, smooth)
     winds = swap(smooth)

time: 94.9 us -> 95.1 us (level)
  the two profiles are of different devices: /device:TPU:40 before, /device:TPU:56 now
where the time goes in v3:
time: 95.1 us; the launch traced here: 94.5 us
  waiting for transfers between devices  43.7 us (46%)
  starting transfers between devices  36.9 us (39%)
  Pallas kernels  11.4 us (12%)
  local copies, waits for them, and re-layouts  1.47 us (2%)
  between operations  0.98 us (1%)
    all_to_all x3, waiting for transfers between devices, swap(): lax.all_to_all(blocks, 'lon', split_axis=0, concat_axis=0, tiled=True)  26 us
    all_to_all x3, starting transfers between devices, swap(): lax.all_to_all(blocks, 'lon', split_axis=0, concat_axis=0, tiled=True)  23.5 us
    ppermute x1, waiting for transfers between devices, shards(): east = lax.ppermute(east, 'lon', east_to_west)  13.4 us
    ppermute x1, starting transfers between devices, shards(): east = lax.ppermute(east, 'lon', east_to_west)  8.06 us
    ppermute x1, waiting for transfers between devices, shards(): south = lax.ppermute(to_north, 'lat', south_to_north)  4.21 us
    ppermute x1, starting transfers between devices, shards(): north = lax.ppermute(to_south, 'lat', north_to_south)  3.31 us
    pallas_call x1, Pallas kernels, shards(): pl.pallas_call(substep_kernel, grid=(levels // step,), in_specs=[pl.Block...  3.06 us
    pallas_call x1, Pallas kernels, shards(): pl.pallas_call(filter_v_kernel, in_specs=[in_vmem] * 15 + [in_hbm], out_s...  2.53 us
  transfers between devices with their start and end apart: 6, of which 5 were waited for; matrix products, arithmetic and copies ran while one was open for 1% of the time, Pallas kernels for 6%

profile of v3, /device:TPU:56, one launch (start us, length us, event | category | flops | bytes accessed | tf_op | source)
XLA Modules:
  0.0 94.5 jit_solution(15866738458322278485)
XLA Ops:
  0.6 12.9 %all-to-all-start.1 = ((f32[16,64,128]{2,1,0:T(8,128)}), f32[16,64,128]{2,1,0:T(8,128)S(1)}, u32[]{:S(2)}, u32[]{:S(2)}) async-start(f32[16,64,128]{2,1,0:T(8,128)} %u_ref.1), calls=%async_computation.1 | async-start | bytes 1048576 | tf_op jit(solution)/shard_map/all_to_all | solution.py:337
  13.5 1.8 %shard_map.201 = (f32[5,16,128]{2,1,0:T(8,128)}, f32[16,128]{1,0:T(8,128)}) custom-call(f32[16,64,128]{2,1,0:T(8,128)} %u_ref.1, f32[16,64,128]{2,1,0:T(8,128)} %v_ref.1, f32[16,64,128]{2,1,0:T(8,128)} %v_ref.1, f32[16,64,128]{2,1,0:T(8,128)} %thick_ref.3, f32[16,64,128]{2,1,0:T(8,128)} %theta_ref.3, f32[16,64,128]{2,1,0:T(8,128)} %traj_ref.3, ...), custom_call_target="tpu_custom_call" | custom-call | tf_op jit(solution)/shard_map/pallas_call | solution.py:362
  15.3 3.3 %collective-permute-start.1 = (f32[5,16,128]{2,1,0:T(8,128)}, f32[5,16,128]{2,1,0:T(8,128)S(1)}, u32[]{:S(2)}, u32[]{:S(2)}) collective-permute-start(f32[5,16,128]{2,1,0:T(8,128)} %get-tuple-element.11), channel_id=1, source_target_pairs={{16,0},{32,16},{48,32},{64,48},{80,64},{96,80},{112,96},{128,112},... | collective-permute-start | bytes 122888 | tf_op jit(solution)/shard_map/ppermute | solution.py:373
  18.8 2.1 %collective-permute-start = (f32[16,128]{1,0:T(8,128)}, f32[16,128]{1,0:T(8,128)S(1)}, u32[]{:S(2)}, u32[]{:S(2)}) collective-permute-start(f32[16,128]{1,0:T(8,128)} %get-tuple-element.10), channel_id=1, source_target_pairs={{0,16},{16,32},{32,48},{48,64},{64,80},{80,96},{96,112},{112,128},... | collective-permute-start | bytes 24584 | tf_op jit(solution)/shard_map/ppermute | solution.py:374
  20.8 4.2 %collective-permute-done.south_ref = f32[16,128]{1,0:T(8,128)S(1)} collective-permute-done((f32[16,128]{1,0:T(8,128)}, f32[16,128]{1,0:T(8,128)S(1)}, u32[]{:S(2)}, u32[]{:S(2)}) %collective-permute-start) | collective-permute-done | bytes 8224 | tf_op jit(solution)/shard_map/ppermute | solution.py:374
  25.0 0.9 shard_map.202
  25.9 3.3 %all-to-all-done.1.x_ref = f32[16,64,128]{2,1,0:T(8,128)S(1)} async-done(((f32[16,64,128]{2,1,0:T(8,128)}), f32[16,64,128]{2,1,0:T(8,128)S(1)}, u32[]{:S(2)}, u32[]{:S(2)}) %all-to-all-start.1) | async-done | bytes 524320 | tf_op jit(solution)/shard_map/all_to_all | solution.py:337
  29.2 6.3 %all-to-all-start = ((f32[16,72,128]{2,1,0:T(8,128)}), f32[16,72,128]{2,1,0:T(8,128)S(1)}, u32[]{:S(2)}, u32[]{:S(2)}) async-start(f32[16,72,128]{2,1,0:T(8,128)} %shard_map.202), calls=%async_computation | async-start | bytes 1179648 | tf_op jit(solution)/shard_map/all_to_all | solution.py:337
  35.5 0.9 shard_map.203
  36.5 0.1 stack_broadcast_in_dim.5
  36.6 0.1 stack_broadcast_in_dim.4
  36.8 2.3 %shard_map.204 = (f32[16,136,128]{2,1,0:T(8,128)}, f32[64,128]{1,0:T(8,128)S(1)}) custom-call(f32[16,64,128]{2,1,0:T(8,128)S(1)} %all-to-all-done.1.x_ref, f32[72,128]{1,0:T(8,128)S(1)} %get-tuple-element.12.limit_ref, f32[72,128]{1,0:T(8,128)S(1)} %get-tuple-element.13.flag_ref, f32[2,7,128]{2,1,0:T(8,128)S(1)} %copy-done.14, f32[2,8,256]{2,1,0:T(8,128)S(1)} %copy-done.13, ...), custom_call_target="tpu_custom_call" | custom-call | tf_op jit(solution)/shard_map/pallas_call | solution.py:417
  39.0 17.1 %all-to-all-done.x_ref = f32[16,72,128]{2,1,0:T(8,128)S(1)} async-done(((f32[16,72,128]{2,1,0:T(8,128)}), f32[16,72,128]{2,1,0:T(8,128)S(1)}, u32[]{:S(2)}, u32[]{:S(2)}) %all-to-all-start) | async-done | bytes 589856 | tf_op jit(solution)/shard_map/all_to_all | solution.py:337
  56.1 2.5 %shard_map.205 = f32[16,136,128]{2,1,0:T(8,128)} custom-call(f32[16,72,128]{2,1,0:T(8,128)S(1)} %all-to-all-done.x_ref, f32[72,128]{1,0:T(8,128)S(1)} %get-tuple-element.12.limit_ref, f32[72,128]{1,0:T(8,128)S(1)} %get-tuple-element.13.flag_ref, f32[2,72,128]{2,1,0:T(8,128)S(1)} %pad_maximum_fusion.geo_ref, ...), custom_call_target="tpu_custom_call", output_to_operand_aliasing={{}: (15, {})} | custom-call | tf_op jit(solution)/shard_map/pallas_call | solution.py:425
  58.7 4.3 %all-to-all-start.2 = ((f32[16,136,128]{2,1,0:T(8,128)}), f32[16,136,128]{2,1,0:T(8,128)S(1)}, u32[]{:S(2)}, u32[]{:S(2)}) async-start(f32[16,136,128]{2,1,0:T(8,128)} %shard_map.205), calls=%async_computation.2 | async-start | bytes 2228224 | tf_op jit(solution)/shard_map/all_to_all | solution.py:337
  63.0 0.2 copy.32
  63.2 0.2 copy.31
  63.4 0.2 copy.30
  63.6 0.4 copy-done.2
  64.0 0.2 copy.33
  64.2 8.1 %collective-permute-start.2 = (f32[3,16,128]{2,1,0:T(8,128)S(1)}, f32[3,16,128]{2,1,0:T(8,128)S(1)}, u32[]{:S(2)}, u32[]{:S(2)}) collective-permute-start(f32[3,16,128]{2,1,0:T(8,128)S(1)} %select_maximum_fusion), channel_id=1, source_target_pairs={{1,0},{2,1},{3,2},{4,3},{5,4},{6,5},{7,6},{8,7},{9,8},{10,9},{11,1... | collective-permute-start | bytes 73736 | tf_op jit(solution)/shard_map/ppermute | solution.py:396
  72.3 13.4 %collective-permute-done.2 = f32[3,16,128]{2,1,0:T(8,128)S(1)} collective-permute-done((f32[3,16,128]{2,1,0:T(8,128)S(1)}, f32[3,16,128]{2,1,0:T(8,128)S(1)}, u32[]{:S(2)}, u32[]{:S(2)}) %collective-permute-start.2) | collective-permute-done | bytes 24608 | tf_op jit(solution)/shard_map/ppermute | solution.py:396
  85.8 5.7 %all-to-all-done.2.winds_ref = f32[16,136,128]{2,1,0:T(8,128)S(1)} async-done(((f32[16,136,128]{2,1,0:T(8,128)}), f32[16,136,128]{2,1,0:T(8,128)S(1)}, u32[]{:S(2)}, u32[]{:S(2)}) %all-to-all-start.2) | async-done | bytes 1114144 | tf_op jit(solution)/shard_map/all_to_all | solution.py:337
  91.5 3.1 %shard_map.206 = (f32[16,64,128]{2,1,0:T(8,128)}, f32[16,64,128]{2,1,0:T(8,128)}, f32[16,64,128]{2,1,0:T(8,128)}, f32[16,64,128]{2,1,0:T(8,128)}) custom-call(f32[16,136,128]{2,1,0:T(8,128)S(1)} %all-to-all-done.2.winds_ref, f32[16,64,128]{2,1,0:T(8,128)S(1)} %copy-done.1, f32[16,64,128]{2,1,0:T(8,128)S(1)} %copy-done.2, f32[16,64,128]{2,1,0:T(8,128)S(1)} %copy-done.3, ...), custom_call_target="tpu_custom_call" | custom-call | tf_op jit(solution)/shard_map/pallas_call | solution.py:440
  (38 shorter events, 0.2 us)
Async XLA Ops:
  0.6 28.5 %all-to-all-start.1 = ((f32[16,64,128]{2,1,0:T(8,128)}), f32[16,64,128]{2,1,0:T(8,128)S(1)}, u32[]{:S(2)}, u32[]{:S(2)}) async-start(f32[16,64,128]{2,1,0:T(8,128)} %u_ref.1), calls=%async_computation.1 | async-start | bytes 1048576 | tf_op jit(solution)/shard_map/all_to_all | solution.py:337
  13.5 11.5 %copy-start = (f32[16,64,128]{2,1,0:T(8,128)S(1)}, f32[16,64,128]{2,1,0:T(8,128)}, u32[]{:S(2)}) copy-start(f32[16,64,128]{2,1,0:T(8,128)} %v_ref.1) | copy-start | bytes 1572868
  15.3 9.7 %collective-permute-start.1 = (f32[5,16,128]{2,1,0:T(8,128)}, f32[5,16,128]{2,1,0:T(8,128)S(1)}, u32[]{:S(2)}, u32[]{:S(2)}) collective-permute-start(f32[5,16,128]{2,1,0:T(8,128)} %get-tuple-element.11), channel_id=1, source_target_pairs={{16,0},{32,16},{48,32},{64,48},{80,64},{96,80},{112,96},{128,112},... | collective-permute-start | bytes 122888 | tf_op jit(solution)/shard_map/ppermute | solution.py:373
  18.6 16.9 %copy-start.15 = (s32[2048]{0:T(1024)S(1)}, s32[2048]{0:T(1024)}, u32[]{:S(2)}) copy-start(s32[2048]{0:T(1024)} %limits_ref.1) | copy-start | bytes 24580
  18.6 16.9 %copy-start.16 = (s32[2048]{0:T(1024)S(1)}, s32[2048]{0:T(1024)}, u32[]{:S(2)}) copy-start(s32[2048]{0:T(1024)} %flags_ref.1) | copy-start | bytes 24580
  18.6 18.0 %copy-start.5 = (bf16[256,256]{1,0:T(8,128)(2,1)S(1)}, bf16[256,256]{1,0:T(8,128)(2,1)}, u32[]{:S(2)}) copy-start(bf16[256,256]{1,0:T(8,128)(2,1)} %constant.55.clone.rest_7_) | copy-start | bytes 393220
  18.6 18.0 %copy-start.6 = (bf16[256,256]{1,0:T(8,128)(2,1)S(1)}, bf16[256,256]{1,0:T(8,128)(2,1)}, u32[]{:S(2)}) copy-start(bf16[256,256]{1,0:T(8,128)(2,1)} %constant.54.clone.rest_6_) | copy-start | bytes 393220
  18.7 18.0 %copy-start.7 = (bf16[256,256]{1,0:T(8,128)(2,1)S(1)}, bf16[256,256]{1,0:T(8,128)(2,1)}, u32[]{:S(2)}) copy-start(bf16[256,256]{1,0:T(8,128)(2,1)} %constant.53.clone.rest_5_) | copy-start | bytes 393220
  18.7 18.0 %copy-start.8 = (bf16[256,256]{1,0:T(8,128)(2,1)S(1)}, bf16[256,256]{1,0:T(8,128)(2,1)}, u32[]{:S(2)}) copy-start(bf16[256,256]{1,0:T(8,128)(2,1)} %constant.52.clone.rest_4_) | copy-start | bytes 393220
  18.7 18.0 %copy-start.9 = (bf16[256,256]{1,0:T(8,128)(2,1)S(1)}, bf16[256,256]{1,0:T(8,128)(2,1)}, u32[]{:S(2)}) copy-start(bf16[256,256]{1,0:T(8,128)(2,1)} %constant.51.clone.rest_3_) | copy-start | bytes 393220
  18.7 18.0 %copy-start.10 = (bf16[256,256]{1,0:T(8,128)(2,1)S(1)}, bf16[256,256]{1,0:T(8,128)(2,1)}, u32[]{:S(2)}) copy-start(bf16[256,256]{1,0:T(8,128)(2,1)} %constant.50.clone.rest_2_) | copy-start | bytes 393220
  18.7 18.0 %copy-start.11 = (bf16[256,256]{1,0:T(8,128)(2,1)S(1)}, bf16[256,256]{1,0:T(8,128)(2,1)}, u32[]{:S(2)}) copy-start(bf16[256,256]{1,0:T(8,128)(2,1)} %constant.49.clone.rest_1_) | copy-start | bytes 393220
  18.7 18.0 %copy-start.12 = (bf16[256,256]{1,0:T(8,128)(2,1)S(1)}, bf16[256,256]{1,0:T(8,128)(2,1)}, u32[]{:S(2)}) copy-start(bf16[256,256]{1,0:T(8,128)(2,1)} %constant.48.clone.rest_0_) | copy-start | bytes 393220
  18.7 18.0 %copy-start.13 = (f32[2,8,256]{2,1,0:T(8,128)S(1)}, f32[2,8,256]{2,1,0:T(8,128)}, u32[]{:S(2)}) copy-start(f32[2,8,256]{2,1,0:T(8,128)} %constant.57.clone.weight_ref) | copy-start | bytes 49156
  18.7 18.0 %copy-start.14 = (f32[2,7,128]{2,1,0:T(8,128)S(1)}, f32[2,7,128]{2,1,0:T(8,128)}, u32[]{:S(2)}) copy-start(f32[2,7,128]{2,1,0:T(8,128)} %constant.56.clone.twist_ref) | copy-start | bytes 21508
  18.8 6.3 %collective-permute-start = (f32[16,128]{1,0:T(8,128)}, f32[16,128]{1,0:T(8,128)S(1)}, u32[]{:S(2)}, u32[]{:S(2)}) collective-permute-start(f32[16,128]{1,0:T(8,128)} %get-tuple-element.10), channel_id=1, source_target_pairs={{0,16},{16,32},{32,48},{48,64},{64,80},{80,96},{96,112},{112,128},... | collective-permute-start | bytes 24584 | tf_op jit(solution)/shard_map/ppermute | solution.py:374
  29.2 27.0 %all-to-all-start = ((f32[16,72,128]{2,1,0:T(8,128)}), f32[16,72,128]{2,1,0:T(8,128)S(1)}, u32[]{:S(2)}, u32[]{:S(2)}) async-start(f32[16,72,128]{2,1,0:T(8,128)} %shard_map.202), calls=%async_computation | async-start | bytes 1179648 | tf_op jit(solution)/shard_map/all_to_all | solution.py:337
  58.7 4.3 %copy-start.4 = (f32[16,64,128]{2,1,0:T(8,128)S(1)}, f32[16,64,128]{2,1,0:T(8,128)}, u32[]{:S(2)}) copy-start(f32[16,64,128]{2,1,0:T(8,128)} %depth_ref.3) | copy-start | bytes 1572868
  58.7 4.5 %copy-start.3 = (f32[16,64,128]{2,1,0:T(8,128)S(1)}, f32[16,64,128]{2,1,0:T(8,128)}, u32[]{:S(2)}) copy-start(f32[16,64,128]{2,1,0:T(8,128)} %traj_ref.3) | copy-start | bytes 1572868
  58.7 4.7 %copy-start.1 = (f32[16,64,128]{2,1,0:T(8,128)S(1)}, f32[16,64,128]{2,1,0:T(8,128)}, u32[]{:S(2)}) copy-start(f32[16,64,128]{2,1,0:T(8,128)} %thick_ref.3) | copy-start | bytes 1572868
  58.7 32.8 %all-to-all-start.2 = ((f32[16,136,128]{2,1,0:T(8,128)}), f32[16,136,128]{2,1,0:T(8,128)S(1)}, u32[]{:S(2)}, u32[]{:S(2)}) async-start(f32[16,136,128]{2,1,0:T(8,128)} %shard_map.205), calls=%async_computation.2 | async-start | bytes 2228224 | tf_op jit(solution)/shard_map/all_to_all | solution.py:337
  63.0 1.0 %copy-start.2 = (f32[16,64,128]{2,1,0:T(8,128)S(1)}, f32[16,64,128]{2,1,0:T(8,128)}, u32[]{:S(2)}) copy-start(f32[16,64,128]{2,1,0:T(8,128)} %theta_ref.3) | copy-start | bytes 1572868
  64.2 21.5 %collective-permute-start.2 = (f32[3,16,128]{2,1,0:T(8,128)S(1)}, f32[3,16,128]{2,1,0:T(8,128)S(1)}, u32[]{:S(2)}, u32[]{:S(2)}) collective-permute-start(f32[3,16,128]{2,1,0:T(8,128)S(1)} %select_maximum_fusion), channel_id=1, source_target_pairs={{1,0},{2,1},{3,2},{4,3},{5,4},{6,5},{7,6},{8,7},{9,8},{10,9},{11,1... | collective-permute-start | bytes 73736 | tf_op jit(solution)/shard_map/ppermute | solution.py:396

commit v4 on v3

--- a/solution.py
+++ b/solution.py
@@ -42,7 +42,7 @@
         matrix = matrix.astype(np.float32)
         high = matrix.astype(jnp.bfloat16)
         low = (matrix - high.astype(np.float32)).astype(jnp.bfloat16)
-        return [jnp.asarray(high), jnp.asarray(low)]
+        return [jnp.asarray(np.concatenate([high, high, low]))]
 
     matrices = split(forward) + split(real_forward) + split(forward.T) + split(real_forward.T)
     return (
@@ -52,14 +52,11 @@
     )
 
 
-def split_product(values, high_ref, low_ref):
+def split_product(values, stacked_ref):
     high = values.astype(jnp.bfloat16)
     low = (values - high.astype(jnp.float32)).astype(jnp.bfloat16)
-    product = functools.partial(jnp.dot, preferred_element_type=jnp.float32)
-    return (
-        product(high, high_ref[...])
-        + (product(low, high_ref[...]) + product(high, low_ref[...]))
-    )
+    parts = jnp.concatenate([high, low, high], axis=1)
+    return jnp.dot(parts, stacked_ref[...], preferred_element_type=jnp.float32)
 
 
 A1, B1, G1 = (float(np.cos(np.pi / 8)), float(np.cos(np.pi / 4)), float(np.cos(3 * np.pi / 8)))
@@ -115,7 +112,7 @@
     segments, rows, width = x_ref.shape
     half = segments // 2
     base = ceil_to((half - 1) * rows, 16)
-    forward, forward_low, real, real_low, back, back_low, real_back, real_back_low = matrices
+    forward, real, back, real_back = matrices
     group = PAD_ROWS
 
     @pl.loop(0, rows // group)
@@ -140,14 +137,14 @@
     def weights(c):
         return jnp.minimum(weight_ref[0, c : c + 1, :], limit * weight_ref[1, c : c + 1, :])
 
-    spectrum = split_product(work_ref[:base, :], forward, forward_low)
+    spectrum = split_product(work_ref[:base, :], forward)
     damping = [weights(c) for c in range(1, half)]
     if base > (half - 1) * rows:
         damping.append(jnp.zeros((base - (half - 1) * rows, 2 * width), jnp.float32))
     spectrum = spectrum * jnp.concatenate(damping, axis=0)
-    work_ref[:base, :] = split_product(spectrum, back, back_low)
-    spectrum = split_product(work_ref[base : base + rows, :], real, real_low) * weights(0)
-    work_ref[base : base + rows, :] = split_product(spectrum, real_back, real_back_low)
+    work_ref[:base, :] = split_product(spectrum, back)
+    spectrum = split_product(work_ref[base : base + rows, :], real) * weights(0)
+    work_ref[base : base + rows, :] = split_product(spectrum, real_back)
 
     def finish(at):
         here = pl.ds(at, group)
@@ -224,7 +221,7 @@
 
 
 def filter_u_kernel(x_ref, limit_ref, flag_ref, twist_ref, weight_ref, *rest):
-    matrices, (out_ref, side_ref, smooth_ref, work_ref, sem) = rest[:8], rest[8:]
+    matrices, (out_ref, side_ref, smooth_ref, work_ref, sem) = rest[:4], rest[4:]
     segments, rows, width = x_ref.shape
     filter_body(x_ref, limit_ref, flag_ref, twist_ref, weight_ref, matrices, smooth_ref, work_ref)
     copy = pltpu.make_async_copy(smooth_ref, out_ref.at[:, :rows, :], sem)
@@ -238,7 +235,7 @@
 
 
 def filter_v_kernel(x_ref, limit_ref, flag_ref, geo_ref, side_ref, twist_ref, weight_ref, *rest):
-    matrices, (_, out_ref, smooth_ref, work_ref, sem) = rest[:8], rest[8:]
+    matrices, (_, out_ref, smooth_ref, work_ref, sem) = rest[:4], rest[4:]
     segments, tall, width = x_ref.shape
     rows = tall - PAD_ROWS
 
@@ -416,7 +413,7 @@
 
     smooth, side = pl.pallas_call(
         filter_u_kernel,
-        in_specs=[in_vmem] * 13,
+        in_specs=[in_vmem] * 9,
         out_specs=[in_hbm, in_vmem],
         out_shape=[hbm(segments, whole_block, width), f32(rows, LANES)],
         scratch_shapes=scratch(rows, pltpu.SemaphoreType.DMA),
@@ -424,10 +421,10 @@
     )(circles_u, limit, flag, twist, weight, *matrices)
     smooth = pl.pallas_call(
         filter_v_kernel,
-        in_specs=[in_vmem] * 15 + [in_hbm],
+        in_specs=[in_vmem] * 11 + [in_hbm],
         out_specs=in_hbm,
         out_shape=hbm(segments, whole_block, width),
-        input_output_aliases={15: 0},
+        input_output_aliases={11: 0},
         scratch_shapes=scratch(tall, pltpu.SemaphoreType.DMA((tall // PAD_ROWS,))),
         compiler_params=params,
     )(circles_v, limit, flag, geo, side, twist, weight, *matrices, smooth)

time: 95.1 us -> 95.1 us (level)
  no operation moved by 1% of the time
where the time goes in v4:
time: 95.1 us; the launch traced here: 94.5 us
  waiting for transfers between devices  43.8 us (46%)
  starting transfers between devices  36.9 us (39%)
  Pallas kernels  11.4 us (12%)
  local copies, waits for them, and re-layouts  1.44 us (2%)
    all_to_all x3, waiting for transfers between devices, swap(): lax.all_to_all(blocks, 'lon', split_axis=0, concat_axis=0, tiled=True)  26.2 us
    all_to_all x3, starting transfers between devices, swap(): lax.all_to_all(blocks, 'lon', split_axis=0, concat_axis=0, tiled=True)  23.5 us
    ppermute x1, waiting for transfers between devices, shards(): east = lax.ppermute(east, 'lon', east_to_west)  13.4 us
    ppermute x1, starting transfers between devices, shards(): east = lax.ppermute(east, 'lon', east_to_west)  8.06 us
    ppermute x1, waiting for transfers between devices, shards(): south = lax.ppermute(to_north, 'lat', south_to_north)  4.19 us
    ppermute x1, starting transfers between devices, shards(): north = lax.ppermute(to_south, 'lat', north_to_south)  3.31 us
    pallas_call x1, Pallas kernels, shards(): pl.pallas_call(substep_kernel, grid=(levels // step,), in_specs=[pl.Block...  3.06 us
    pallas_call x1, Pallas kernels, shards(): pl.pallas_call(filter_v_kernel, in_specs=[in_vmem] * 11 + [in_hbm], out_s...  2.54 us
  transfers between devices with their start and end apart: 6, of which 5 were waited for; matrix products, arithmetic and copies ran while one was open for 1% of the time, Pallas kernels for 6%

profile of v4, /device:TPU:56, one launch (start us, length us, event | category | flops | bytes accessed | tf_op | source)
XLA Modules:
  0.0 94.5 jit_solution(15132129252309357096)
XLA Ops:
  0.6 12.9 %all-to-all-start.1 = ((f32[16,64,128]{2,1,0:T(8,128)}), f32[16,64,128]{2,1,0:T(8,128)S(1)}, u32[]{:S(2)}, u32[]{:S(2)}) async-start(f32[16,64,128]{2,1,0:T(8,128)} %u_ref.1), calls=%async_computation.1 | async-start | bytes 1048576 | tf_op jit(solution)/shard_map/all_to_all | solution.py:334
  13.5 1.8 %shard_map.165 = (f32[5,16,128]{2,1,0:T(8,128)}, f32[16,128]{1,0:T(8,128)}) custom-call(f32[16,64,128]{2,1,0:T(8,128)} %u_ref.1, f32[16,64,128]{2,1,0:T(8,128)} %v_ref.1, f32[16,64,128]{2,1,0:T(8,128)} %v_ref.1, f32[16,64,128]{2,1,0:T(8,128)} %thick_ref.3, f32[16,64,128]{2,1,0:T(8,128)} %theta_ref.3, f32[16,64,128]{2,1,0:T(8,128)} %traj_ref.3, ...), custom_call_target="tpu_custom_call" | custom-call | tf_op jit(solution)/shard_map/pallas_call | solution.py:359
  15.3 3.3 %collective-permute-start.1 = (f32[5,16,128]{2,1,0:T(8,128)}, f32[5,16,128]{2,1,0:T(8,128)S(1)}, u32[]{:S(2)}, u32[]{:S(2)}) collective-permute-start(f32[5,16,128]{2,1,0:T(8,128)} %get-tuple-element.11), channel_id=1, source_target_pairs={{16,0},{32,16},{48,32},{64,48},{80,64},{96,80},{112,96},{128,112},... | collective-permute-start | bytes 122888 | tf_op jit(solution)/shard_map/ppermute | solution.py:370
  18.7 2.1 %collective-permute-start = (f32[16,128]{1,0:T(8,128)}, f32[16,128]{1,0:T(8,128)S(1)}, u32[]{:S(2)}, u32[]{:S(2)}) collective-permute-start(f32[16,128]{1,0:T(8,128)} %get-tuple-element.10), channel_id=1, source_target_pairs={{0,16},{16,32},{32,48},{48,64},{64,80},{80,96},{96,112},{112,128},... | collective-permute-start | bytes 24584 | tf_op jit(solution)/shard_map/ppermute | solution.py:371
  20.8 4.2 %collective-permute-done.south_ref = f32[16,128]{1,0:T(8,128)S(1)} collective-permute-done((f32[16,128]{1,0:T(8,128)}, f32[16,128]{1,0:T(8,128)S(1)}, u32[]{:S(2)}, u32[]{:S(2)}) %collective-permute-start) | collective-permute-done | bytes 8224 | tf_op jit(solution)/shard_map/ppermute | solution.py:371
  25.0 0.9 shard_map.166
  25.8 3.3 %all-to-all-done.1.x_ref = f32[16,64,128]{2,1,0:T(8,128)S(1)} async-done(((f32[16,64,128]{2,1,0:T(8,128)}), f32[16,64,128]{2,1,0:T(8,128)S(1)}, u32[]{:S(2)}, u32[]{:S(2)}) %all-to-all-start.1) | async-done | bytes 524320 | tf_op jit(solution)/shard_map/all_to_all | solution.py:334
  29.2 6.3 %all-to-all-start = ((f32[16,72,128]{2,1,0:T(8,128)}), f32[16,72,128]{2,1,0:T(8,128)S(1)}, u32[]{:S(2)}, u32[]{:S(2)}) async-start(f32[16,72,128]{2,1,0:T(8,128)} %shard_map.166), calls=%async_computation | async-start | bytes 1179648 | tf_op jit(solution)/shard_map/all_to_all | solution.py:334
  35.5 0.9 shard_map.167
  36.5 0.1 stack_broadcast_in_dim.5
  36.6 0.1 stack_broadcast_in_dim.4
  36.7 2.3 %shard_map.168 = (f32[16,136,128]{2,1,0:T(8,128)}, f32[64,128]{1,0:T(8,128)S(1)}) custom-call(f32[16,64,128]{2,1,0:T(8,128)S(1)} %all-to-all-done.1.x_ref, f32[72,128]{1,0:T(8,128)S(1)} %get-tuple-element.12.limit_ref, f32[72,128]{1,0:T(8,128)S(1)} %get-tuple-element.13.flag_ref, f32[2,7,128]{2,1,0:T(8,128)S(1)} %copy-done.10, f32[2,8,256]{2,1,0:T(8,128)S(1)} %copy-done.9, ...), custom_call_target="tpu_custom_call" | custom-call | tf_op jit(solution)/shard_map/pallas_call | solution.py:414
  39.0 17.1 %all-to-all-done.x_ref = f32[16,72,128]{2,1,0:T(8,128)S(1)} async-done(((f32[16,72,128]{2,1,0:T(8,128)}), f32[16,72,128]{2,1,0:T(8,128)S(1)}, u32[]{:S(2)}, u32[]{:S(2)}) %all-to-all-start) | async-done | bytes 589856 | tf_op jit(solution)/shard_map/all_to_all | solution.py:334
  56.1 2.5 %shard_map.169 = f32[16,136,128]{2,1,0:T(8,128)} custom-call(f32[16,72,128]{2,1,0:T(8,128)S(1)} %all-to-all-done.x_ref, f32[72,128]{1,0:T(8,128)S(1)} %get-tuple-element.12.limit_ref, f32[72,128]{1,0:T(8,128)S(1)} %get-tuple-element.13.flag_ref, f32[2,72,128]{2,1,0:T(8,128)S(1)} %pad_maximum_fusion.geo_ref, ...), custom_call_target="tpu_custom_call", output_to_operand_aliasing={{}: (11, {})} | custom-call | tf_op jit(solution)/shard_map/pallas_call | solution.py:422
  58.7 4.3 %all-to-all-start.2 = ((f32[16,136,128]{2,1,0:T(8,128)}), f32[16,136,128]{2,1,0:T(8,128)S(1)}, u32[]{:S(2)}, u32[]{:S(2)}) async-start(f32[16,136,128]{2,1,0:T(8,128)} %shard_map.169), calls=%async_computation.2 | async-start | bytes 2228224 | tf_op jit(solution)/shard_map/all_to_all | solution.py:334
  63.0 0.2 copy.28
  63.2 0.2 copy.27
  63.5 0.2 copy.26
  63.7 0.4 copy-done.2
  64.1 0.2 copy.29
  64.3 8.1 %collective-permute-start.2 = (f32[3,16,128]{2,1,0:T(8,128)S(1)}, f32[3,16,128]{2,1,0:T(8,128)S(1)}, u32[]{:S(2)}, u32[]{:S(2)}) collective-permute-start(f32[3,16,128]{2,1,0:T(8,128)S(1)} %select_maximum_fusion), channel_id=1, source_target_pairs={{1,0},{2,1},{3,2},{4,3},{5,4},{6,5},{7,6},{8,7},{9,8},{10,9},{11,1... | collective-permute-start | bytes 73736 | tf_op jit(solution)/shard_map/ppermute | solution.py:393
  72.4 13.4 %collective-permute-done.2 = f32[3,16,128]{2,1,0:T(8,128)S(1)} collective-permute-done((f32[3,16,128]{2,1,0:T(8,128)S(1)}, f32[3,16,128]{2,1,0:T(8,128)S(1)}, u32[]{:S(2)}, u32[]{:S(2)}) %collective-permute-start.2) | collective-permute-done | bytes 24608 | tf_op jit(solution)/shard_map/ppermute | solution.py:393
  85.7 5.7 %all-to-all-done.2.winds_ref = f32[16,136,128]{2,1,0:T(8,128)S(1)} async-done(((f32[16,136,128]{2,1,0:T(8,128)}), f32[16,136,128]{2,1,0:T(8,128)S(1)}, u32[]{:S(2)}, u32[]{:S(2)}) %all-to-all-start.2) | async-done | bytes 1114144 | tf_op jit(solution)/shard_map/all_to_all | solution.py:334
  91.5 3.1 %shard_map.170 = (f32[16,64,128]{2,1,0:T(8,128)}, f32[16,64,128]{2,1,0:T(8,128)}, f32[16,64,128]{2,1,0:T(8,128)}, f32[16,64,128]{2,1,0:T(8,128)}) custom-call(f32[16,136,128]{2,1,0:T(8,128)S(1)} %all-to-all-done.2.winds_ref, f32[16,64,128]{2,1,0:T(8,128)S(1)} %copy-done.1, f32[16,64,128]{2,1,0:T(8,128)S(1)} %copy-done.2, f32[16,64,128]{2,1,0:T(8,128)S(1)} %copy-done.3, ...), custom_call_target="tpu_custom_call" | custom-call | tf_op jit(solution)/shard_map/pallas_call | solution.py:437
  (30 shorter events, 0.2 us)
Async XLA Ops:
  0.6 28.5 %all-to-all-start.1 = ((f32[16,64,128]{2,1,0:T(8,128)}), f32[16,64,128]{2,1,0:T(8,128)S(1)}, u32[]{:S(2)}, u32[]{:S(2)}) async-start(f32[16,64,128]{2,1,0:T(8,128)} %u_ref.1), calls=%async_computation.1 | async-start | bytes 1048576 | tf_op jit(solution)/shard_map/all_to_all | solution.py:334
  13.5 11.4 %copy-start = (f32[16,64,128]{2,1,0:T(8,128)S(1)}, f32[16,64,128]{2,1,0:T(8,128)}, u32[]{:S(2)}) copy-start(f32[16,64,128]{2,1,0:T(8,128)} %v_ref.1) | copy-start | bytes 1572868
  15.3 9.7 %collective-permute-start.1 = (f32[5,16,128]{2,1,0:T(8,128)}, f32[5,16,128]{2,1,0:T(8,128)S(1)}, u32[]{:S(2)}, u32[]{:S(2)}) collective-permute-start(f32[5,16,128]{2,1,0:T(8,128)} %get-tuple-element.11), channel_id=1, source_target_pairs={{16,0},{32,16},{48,32},{64,48},{80,64},{96,80},{112,96},{128,112},... | collective-permute-start | bytes 122888 | tf_op jit(solution)/shard_map/ppermute | solution.py:370
  18.6 16.9 %copy-start.11 = (s32[2048]{0:T(1024)S(1)}, s32[2048]{0:T(1024)}, u32[]{:S(2)}) copy-start(s32[2048]{0:T(1024)} %limits_ref.1) | copy-start | bytes 24580
  18.6 16.9 %copy-start.12 = (s32[2048]{0:T(1024)S(1)}, s32[2048]{0:T(1024)}, u32[]{:S(2)}) copy-start(s32[2048]{0:T(1024)} %flags_ref.1) | copy-start | bytes 24580
  18.6 18.0 %copy-start.5 = (bf16[768,256]{1,0:T(8,128)(2,1)S(1)}, bf16[768,256]{1,0:T(8,128)(2,1)}, u32[]{:S(2)}) copy-start(bf16[768,256]{1,0:T(8,128)(2,1)} %constant.43.clone.rest_3_) | copy-start | bytes 1179652
  18.6 18.0 %copy-start.6 = (bf16[768,256]{1,0:T(8,128)(2,1)S(1)}, bf16[768,256]{1,0:T(8,128)(2,1)}, u32[]{:S(2)}) copy-start(bf16[768,256]{1,0:T(8,128)(2,1)} %constant.42.clone.rest_2_) | copy-start | bytes 1179652
  18.7 18.0 %copy-start.7 = (bf16[768,256]{1,0:T(8,128)(2,1)S(1)}, bf16[768,256]{1,0:T(8,128)(2,1)}, u32[]{:S(2)}) copy-start(bf16[768,256]{1,0:T(8,128)(2,1)} %constant.41.clone.rest_1_) | copy-start | bytes 1179652
  18.7 18.0 %copy-start.8 = (bf16[768,256]{1,0:T(8,128)(2,1)S(1)}, bf16[768,256]{1,0:T(8,128)(2,1)}, u32[]{:S(2)}) copy-start(bf16[768,256]{1,0:T(8,128)(2,1)} %constant.40.clone.rest_0_) | copy-start | bytes 1179652
  18.7 18.0 %copy-start.9 = (f32[2,8,256]{2,1,0:T(8,128)S(1)}, f32[2,8,256]{2,1,0:T(8,128)}, u32[]{:S(2)}) copy-start(f32[2,8,256]{2,1,0:T(8,128)} %constant.45.clone.weight_ref) | copy-start | bytes 49156
  18.7 18.0 %copy-start.10 = (f32[2,7,128]{2,1,0:T(8,128)S(1)}, f32[2,7,128]{2,1,0:T(8,128)}, u32[]{:S(2)}) copy-start(f32[2,7,128]{2,1,0:T(8,128)} %constant.44.clone.twist_ref) | copy-start | bytes 21508
  18.7 6.2 %collective-permute-start = (f32[16,128]{1,0:T(8,128)}, f32[16,128]{1,0:T(8,128)S(1)}, u32[]{:S(2)}, u32[]{:S(2)}) collective-permute-start(f32[16,128]{1,0:T(8,128)} %get-tuple-element.10), channel_id=1, source_target_pairs={{0,16},{16,32},{32,48},{48,64},{64,80},{80,96},{96,112},{112,128},... | collective-permute-start | bytes 24584 | tf_op jit(solution)/shard_map/ppermute | solution.py:371
  29.2 27.0 %all-to-all-start = ((f32[16,72,128]{2,1,0:T(8,128)}), f32[16,72,128]{2,1,0:T(8,128)S(1)}, u32[]{:S(2)}, u32[]{:S(2)}) async-start(f32[16,72,128]{2,1,0:T(8,128)} %shard_map.166), calls=%async_computation | async-start | bytes 1179648 | tf_op jit(solution)/shard_map/all_to_all | solution.py:334
  58.7 4.3 %copy-start.4 = (f32[16,64,128]{2,1,0:T(8,128)S(1)}, f32[16,64,128]{2,1,0:T(8,128)}, u32[]{:S(2)}) copy-start(f32[16,64,128]{2,1,0:T(8,128)} %depth_ref.3) | copy-start | bytes 1572868
  58.7 4.5 %copy-start.3 = (f32[16,64,128]{2,1,0:T(8,128)S(1)}, f32[16,64,128]{2,1,0:T(8,128)}, u32[]{:S(2)}) copy-start(f32[16,64,128]{2,1,0:T(8,128)} %traj_ref.3) | copy-start | bytes 1572868
  58.7 4.8 %copy-start.1 = (f32[16,64,128]{2,1,0:T(8,128)S(1)}, f32[16,64,128]{2,1,0:T(8,128)}, u32[]{:S(2)}) copy-start(f32[16,64,128]{2,1,0:T(8,128)} %thick_ref.3) | copy-start | bytes 1572868
  58.7 32.7 %all-to-all-start.2 = ((f32[16,136,128]{2,1,0:T(8,128)}), f32[16,136,128]{2,1,0:T(8,128)S(1)}, u32[]{:S(2)}, u32[]{:S(2)}) async-start(f32[16,136,128]{2,1,0:T(8,128)} %shard_map.169), calls=%async_computation.2 | async-start | bytes 2228224 | tf_op jit(solution)/shard_map/all_to_all | solution.py:334
  63.0 1.0 %copy-start.2 = (f32[16,64,128]{2,1,0:T(8,128)S(1)}, f32[16,64,128]{2,1,0:T(8,128)}, u32[]{:S(2)}) copy-start(f32[16,64,128]{2,1,0:T(8,128)} %theta_ref.3) | copy-start | bytes 1572868
  64.3 21.4 %collective-permute-start.2 = (f32[3,16,128]{2,1,0:T(8,128)S(1)}, f32[3,16,128]{2,1,0:T(8,128)S(1)}, u32[]{:S(2)}, u32[]{:S(2)}) collective-permute-start(f32[3,16,128]{2,1,0:T(8,128)S(1)} %select_maximum_fusion), channel_id=1, source_target_pairs={{1,0},{2,1},{3,2},{4,3},{5,4},{6,5},{7,6},{8,7},{9,8},{10,9},{11,1... | collective-permute-start | bytes 73736 | tf_op jit(solution)/shard_map/ppermute | solution.py:393
